TPU v7x, 256 devices: a whole 4x4x8 slice. The times are simulated.
256 devices in a mesh: dp: 4 (over y), ctx: 64 (over x, z, core).
Axes of the slice: x: 4, y: 4, z: 8, core: 2. Of those that a mesh axis runs over, the one named last changes fastest.
Arguments:
- queries: bfloat16 [4, 8192, 2048], P('dp', 'ctx'), may hold values from -6 to 6
- key_rows: bfloat16 [4, 8192, 2048], P('dp', 'ctx'), may hold values from -6 to 6
- value_rows: bfloat16 [4, 8192, 2048], P('dp', 'ctx'), may hold values from -6 to 6
- out_grad: bfloat16 [4, 8192, 2048], P('dp', 'ctx'), may hold values from -8 to 8
- norm_gain: float32 [2048], replicated, may hold values from 0.1 to 1.9
Outputs:
- query_grad: bfloat16 [4, 8192, 2048], P('dp', 'ctx')
- key_grad: bfloat16 [4, 8192, 2048], P('dp', 'ctx')
- value_grad: bfloat16 [4, 8192, 2048], P('dp', 'ctx')
- gain_grad: float32 [2048], P(('dp', 'ctx'))
All inputs are finite; a program needn't handle non-finite values.
Results may differ from a plain program's by a relative error of at most 0.0065.
Values sent between devices are 32-bit elements; how exact they have to be, the bound alone decides.
A program may use at most 256 MiB of HBM per device.

v0:
```python
import math

import jax
import jax.numpy as jnp
from jax import lax
from jax.sharding import PartitionSpec as P

HEADS = 16
HEAD_DIM = 128


EPSILON = 1e-05
BLOCK_ROWS = 512


def entering(value, axis, join, neutral, backward):
    count, mine = (lax.axis_size(axis), lax.axis_index(axis))
    pieces = lax.all_gather(value, axis)
    if backward:
        pieces = pieces[::-1]
        mine = count - 1 - mine
    running = jnp.full_like(value, 0) + jnp.asarray(neutral, value.dtype)

    def lap(position, running):
        longer = join(running, pieces[position])
        return jnp.where(position < mine, longer, running)

    return lax.fori_loop(0, count - 1, lap, running)


def masked_scores(left_rows, right_rows):
    length = left_rows.shape[0]
    step_rows = min(BLOCK_ROWS, length)
    products = jnp.einsum("lhe,mhe->hlm", left_rows, right_rows, preferred_element_type=jnp.float32)
    rows_idx = 0 + lax.broadcasted_iota(jnp.int32, (step_rows, step_rows), 0)
    cols_idx = lax.broadcasted_iota(jnp.int32, (step_rows, step_rows), 1)
    kept = jnp.where((cols_idx <= rows_idx)[None], products, 0.0).astype(jnp.bfloat16)
    return kept


def add_states(earlier, later_one):
    return earlier + later_one


def body(queries, key_rows, value_rows, out_grad, norm_gain):
    length = queries.shape[1]
    q_rows = queries.reshape(length, HEADS, HEAD_DIM)
    k_rows = key_rows.reshape(length, HEADS, HEAD_DIM)
    v_rows = value_rows.reshape(length, HEADS, HEAD_DIM)
    g_rows = out_grad.reshape(length, HEADS, HEAD_DIM)
    zero_state = jnp.zeros((HEADS, HEAD_DIM, HEAD_DIM), jnp.float32)
    kv_local = jnp.einsum("lhe,lhf->hef", k_rows, v_rows, preferred_element_type=jnp.float32)
    scores_low = masked_scores(q_rows, k_rows)
    prior_state = entering(kv_local, "ctx", add_states, zero_state, False)
    prior_low = prior_state.astype(jnp.bfloat16)
    output = jnp.einsum("hlm,mhf->lhf", scores_low, v_rows, preferred_element_type=jnp.float32)
    output = output + jnp.einsum(
        "lhe,hef->lhf", q_rows, prior_low, preferred_element_type=jnp.float32
    )
    root_mean = jnp.sqrt(jnp.mean(output * output, axis=-1, keepdims=True) + EPSILON)
    normed = output / root_mean
    grad_float = g_rows.astype(jnp.float32)
    grad_normed = grad_float * norm_gain.reshape(HEADS, HEAD_DIM)
    grad_output = (
        (grad_normed - normed * jnp.mean(grad_normed * normed, axis=-1, keepdims=True)) / root_mean
    ).astype(jnp.bfloat16)
    gain_term = jnp.sum(grad_float * normed, axis=0).reshape(HEADS * HEAD_DIM)
    grad_local = jnp.einsum("lhe,lhf->hef", q_rows, grad_output, preferred_element_type=jnp.float32)
    later_state = entering(grad_local, "ctx", add_states, zero_state, True)
    later_low = later_state.astype(jnp.bfloat16)
    grad_scores = masked_scores(grad_output, v_rows)
    query_grad = jnp.einsum("hlm,mhe->lhe", grad_scores, k_rows, preferred_element_type=jnp.float32)
    query_grad = query_grad + jnp.einsum(
        "lhf,hef->lhe", grad_output, prior_low, preferred_element_type=jnp.float32
    )
    key_grad = jnp.einsum("hlm,lhe->mhe", grad_scores, q_rows, preferred_element_type=jnp.float32)
    key_grad = key_grad + jnp.einsum(
        "mhf,hef->mhe", v_rows, later_low, preferred_element_type=jnp.float32
    )
    value_grad = jnp.einsum(
        "hlm,lhf->mhf", scores_low, grad_output, preferred_element_type=jnp.float32
    )
    value_grad = value_grad + jnp.einsum(
        "mhe,hef->mhf", k_rows, later_low, preferred_element_type=jnp.float32
    )
    gain_shard = lax.psum_scatter(gain_term, ("dp", "ctx"), scatter_dimension=0, tiled=True)
    token_count = lax.axis_size("dp") * lax.axis_size("ctx") * length
    gain_grad = gain_shard / math.sqrt(token_count)
    shape_out = (1, length, HEADS * HEAD_DIM)
    return (
        query_grad.astype(jnp.bfloat16).reshape(shape_out),
        key_grad.astype(jnp.bfloat16).reshape(shape_out),
        value_grad.astype(jnp.bfloat16).reshape(shape_out),
        gain_grad,
    )


def solution(mesh):
    placed = (
        P("dp", "ctx", None),
        P("dp", "ctx", None),
        P("dp", "ctx", None),
        P("dp", "ctx", None),
        P(),
    )
    return jax.shard_map(
        body,
        mesh=mesh,
        in_specs=placed,
        out_specs=(
            P("dp", "ctx", None),
            P("dp", "ctx", None),
            P("dp", "ctx", None),
            P(("dp", "ctx")),
        ),
        check_vma=False,
    )
```

profile of v0, /device:TPU:1, one launch (start us, length us, event | category | flops | bytes accessed | tf_op | source)
XLA Modules:
  0.0 755.8 jit_solution(11702991807469588540)
XLA Ops:
  17.9 234.3 %all-gather.5.cloned.1.call-done = f32[1024,128,128]{2,1,0:T(8,128)} async-done(((f32[16,128,128]{2,1,0:T(8,128)}), f32[1024,128,128]{2,1,0:T(8,128)}) %all-gather.5.cloned.1.call-update) | async-done | bytes 67108880 | tf_op jit(solution)/shard_map/all_gather | solution.py:18
  252.2 101.7 %while.28 = (s32[]{:T(128)}, f32[16,128,128]{2,1,0:T(8,128)S(1)}, s32[]{:T(128)}, f32[64,16,128,128]{3,2,1,0:T(8,128)}, s32[]{:T(128)}, /*index=5*/s32[]{:T(128)}) while((s32[]{:T(128)}, f32[16,128,128]{2,1,0:T(8,128)S(1)}, s32[]{:T(128)}, f32[64,16,128,128]{3,2,1,0:T(8,128)}, s32[]{:T(128)}, /*index=5*/s32[]{:T(128)}) %tuple.67), condition=%wide.region_1.2_spmd.clone, body=%wide.region_0.1_spmd.clone.sunk | while | flops 786436 | bytes 3145821 | solution.py:28
  253.8 1.6 add_select_fusion.4
  257.0 1.6 add_select_fusion.4
  260.2 1.6 add_select_fusion.4
  263.5 1.6 add_select_fusion.4
  265.1 1.6 add_select_fusion.4
  266.7 1.6 add_select_fusion.4
  268.3 1.6 add_select_fusion.4
  269.9 1.6 add_select_fusion.4
  271.5 1.6 add_select_fusion.4
  273.1 1.6 add_select_fusion.4
  274.8 1.6 add_select_fusion.4
  278.0 1.6 add_select_fusion.4
  353.8 1.7 multiply_reduce_fusion.2
  362.0 1.7 convolution_bitcast_fusion.4
  363.8 2.1 fusion.5
  365.9 2.0 copy.48
  367.9 76.6 %all-reduce = f32[2048]{0:T(1024)S(1)} all-reduce(f32[2048]{0:T(1024)S(1)} %bitcast.82), channel_id=4, replica_groups=mesh['dp'=4,'ctx'=64] {'dp','ctx'}, use_global_device_ids=true, to_apply=%region_7.8.clone | all-reduce | flops 2048 | bytes 16384
  445.1 2.5 fusion.23
  447.6 148.1 %all-gather.7.cloned.1.call-done = f32[1024,128,128]{2,1,0:T(8,128)} async-done(((f32[16,128,128]{2,1,0:T(8,128)}), f32[1024,128,128]{2,1,0:T(8,128)}) %all-gather.7.cloned.1.call-update) | async-done | bytes 67108880 | tf_op jit(solution)/shard_map/all_gather | solution.py:18
  595.6 44.9 %rev.3 = f32[64,16,128,128]{3,2,1,0:T(8,128)} reverse(f32[64,16,128,128]{3,2,1,0:T(8,128)} %bitcast.10), dimensions={0} | reverse | bytes 134217728 | tf_op jit(solution)/shard_map/rev | solution.py:20
  640.5 101.6 %while.29 = (s32[]{:T(128)}, f32[16,128,128]{2,1,0:T(8,128)S(1)}, s32[]{:T(128)}, f32[64,16,128,128]{3,2,1,0:T(8,128)}, s32[]{:T(128)}, /*index=5*/s32[]{:T(128)}) while((s32[]{:T(128)}, f32[16,128,128]{2,1,0:T(8,128)S(1)}, s32[]{:T(128)}, f32[64,16,128,128]{3,2,1,0:T(8,128)}, s32[]{:T(128)}, /*index=5*/s32[]{:T(128)}) %tuple.70), condition=%wide.region_5.6_spmd.clone, body=%wide.region_4.5_spmd.clone.sunk | while | flops 786436 | bytes 3145821 | solution.py:28
  743.6 1.7 fusion.6
  (155 shorter events, 203.8 us)
Async XLA Ops:
  7.2 245.0 %all-gather.5.cloned.1.call-start = ((), (), s32[]{:S(2)}) async-start(), calls=%async_computation | async-start | bytes 68157440 | tf_op jit(solution)/shard_map/all_gather | solution.py:18
  8.4 3.2 copy-start.1
  10.2 1.4 copy-start.3
  11.5 584.1 %all-gather.7.cloned.1.call-start = ((), (), s32[]{:S(2)}) async-start(), calls=%async_computation.1 | async-start | bytes 68157440 | tf_op jit(solution)/shard_map/all_gather | solution.py:18
  15.5 0.8 copy-start.6
  358.0 0.8 copy-start
  362.0 3.9 copy-start.4
  595.6 148.0 %copy-start.2 = (bf16[16,8,16,128]{3,2,1,0:T(8,128)(2,1)S(1)}, bf16[16,8,16,128]{3,2,1,0:T(8,128)(2,1)}, u32[]{:S(2)}) copy-start(bf16[16,8,16,128]{3,2,1,0:T(8,128)(2,1)} %copy-done.1) | copy-start | bytes 1572868
  595.6 150.8 %copy-start.5 = (bf16[16,128,128]{2,1,0:T(8,128)(2,1)S(1)}, bf16[16,128,128]{2,1,0:T(8,128)(2,1)}, u32[]{:S(2)}) copy-start(bf16[16,128,128]{2,1,0:T(8,128)(2,1)} %copy-done.4) | copy-start | bytes 1572868
Sparse Core Ops, SparseCore 0:
  11.6 240.4 all-gather.4
  360.6 235.0 all-gather.6
where the time goes:
time: 762 us; the launch traced here: 756 us
  waiting for transfers between devices  382 us (50%)
  other arithmetic  203 us (27%)
  blocking collectives  76.6 us (10%)
  local copies, waits for them, and re-layouts  57.2 us (8%)
  matrix products  19 us (2%)
  between operations  14.2 us (2%)
    all_gather x2, waiting for transfers between devices, entering(): pieces = lax.all_gather(value, axis)  382 us
    select_n x126, other arithmetic, lap(): return jnp.where(position < mine, longer, running)  200 us
    unnamed x1, blocking collectives  76.6 us
    rev x1, local copies, waits for them, and re-layouts, entering(): pieces = pieces[::-1]  44.9 us
  transfers between devices with their start and end apart: 2, of which 2 were waited for; matrix products, arithmetic and copies ran while one was open for 2% of the time, Pallas kernels for 0%

commit v1 on v0

v1 whole, which is shorter than its diff:
```python
import functools
import math

import jax
import jax.numpy as jnp
from jax import lax
from jax.experimental import pallas as pl
from jax.experimental.pallas import tpu as pltpu
from jax.sharding import PartitionSpec as P

HEADS = 16
HALF = 8
DIM = 128
EPSILON = 1e-05
MESH = pl.DeviceIdType.MESH
F32 = jnp.float32
BF16 = jnp.bfloat16

CH = 2
HOP = 3
LAG = 2
ROWS = DIM // CH
CHUNKS = HALF * CH


def dot(a, b, ca, cb):
    return lax.dot_general(a, b, (((ca,), (cb,)), ((), ())), preferred_element_type=F32)


class Scan:
    def __init__(self, sizes, pos, order, bufs, sems):
        self.nx, self.nz = sizes
        self.y, self.x, self.z, self.c = pos
        self.order = order
        if order > 0:
            self.px, self.pz, self.pc = self.x, self.z, self.c
        else:
            self.px, self.pz, self.pc = self.nx - 1 - self.x, self.nz - 1 - self.z, 1 - self.c
        (self.own, self.exch, self.xin, self.a, self.upin, self.upout, self.dnin, self.dnout, self.bkin, self.bkout) = bufs
        self.re, self.rx, self.ru, self.rd, self.rb, self.sends = sems

    def device(self, x, z, c):
        return (self.y, (x * self.nz + z) * 2 + c)

    def partner(self):
        return self.device(self.x, self.z, 1 - self.c)

    def remote(self, src, dst, which, recv, to):
        return pltpu.make_async_remote_copy(
            src_ref=src, dst_ref=dst, send_sem=self.sends.at[which], recv_sem=recv, device_id=to, device_id_type=MESH
        )

    def exch_copy(self, m):
        src = self.own.at[pl.ds(((1 - self.c) * HALF + m) * CH, CH)]
        return self.remote(src, self.exch.at[pl.ds(m * CH, CH)], 0, self.re.at[m], self.partner())

    def x_copy(self, j):
        return self.remote(
            self.a.at[j], self.xin.at[j], 1, self.rx.at[j], self.device(self.x + self.order, self.z, self.c)
        )

    def up_copy(self, src, j):
        return self.remote(
            src.at[j], self.upin.at[j], 2, self.ru.at[j], self.device(self.x, self.z + self.order, self.c)
        )

    def dn_copy(self, src, j):
        return self.remote(
            src.at[j], self.dnin.at[j], 3, self.rd.at[j], self.device(self.x, self.z - self.order, self.c)
        )

    def bk_copy(self, m):
        part = pl.ds(m * CH, CH)
        return self.remote(self.bkout.at[part], self.bkin.at[part], 4, self.rb.at[m], self.partner())

    def clear(self):
        @pl.when(self.px == 0)
        def _():
            self.xin[...] = jnp.zeros(self.xin.shape, F32)

        @pl.when(self.pz == 0)
        def _():
            self.upin[...] = jnp.zeros(self.upin.shape, F32)

        @pl.when((self.px == 0) | (self.pz == self.nz - 1))
        def _():
            self.dnin[...] = jnp.zeros(self.dnin.shape, F32)

    def along_x(self, j):
        @pl.when(j % CH == 0)
        def _():
            self.exch_copy(j // CH).wait_recv()

        @pl.when(self.px > 0)
        def _():
            self.x_copy(j).wait_recv()

        self.a[j] = self.own[self.c * CHUNKS + j] + self.exch[j] + self.xin[j]

        @pl.when(self.px < self.nx - 1)
        def _():
            self.x_copy(j).start()

        @pl.when(self.pz == 0)
        def _():
            self.up_copy(self.a, j).start()

        @pl.when((self.pz == self.nz - 1) & (self.px > 0))
        def _():
            self.dn_copy(self.xin, j).start()

    def up(self, j):
        self.up_copy(self.upout, j).wait_recv()

        @pl.when(self.pz < self.nz - 1)
        def _():
            self.upout[j] = self.upin[j] + self.a[j]
            self.up_copy(self.upout, j).start()

    def down(self, j):
        self.dn_copy(self.dnout, j).wait_recv()

        @pl.when(self.pz > 0)
        def _():
            self.dnout[j] = self.dnin[j] + self.xin[j]
            self.dn_copy(self.dnout, j).start()

    def forward(self, t):
        jx = t - HOP * self.px
        ju = jx - HOP * self.pz
        jd = jx - HOP * (self.nz - 1 - self.pz)

        @pl.when((jx >= 0) & (jx < CHUNKS))
        def _():
            self.along_x(jx)

        @pl.when((ju >= 0) & (ju < CHUNKS) & (self.pz > 0))
        def _():
            self.up(ju)

        @pl.when((jd >= 0) & (jd < CHUNKS) & (self.pz < self.nz - 1) & (self.px > 0))
        def _():
            self.down(jd)

    def finish(self, m):
        part = pl.ds(m * CH, CH)
        before = (self.upin[part] + self.xin[part] + self.dnin[part]).reshape(DIM, DIM)
        first = self.own[pl.ds(self.c * CHUNKS + m * CH, CH)].reshape(DIM, DIM)
        second = self.exch[part].reshape(DIM, DIM)
        self.bkout[part] = jnp.where(self.pc == 0, before + first, before).reshape(CH, ROWS, DIM)
        self.bk_copy(m).start()
        return jnp.where(self.pc == 1, before + second, before)

    def finished(self, m):
        self.bk_copy(m).wait_recv()
        return self.bkin[pl.ds(m * CH, CH)].reshape(DIM, DIM)

    def drain(self):
        whole = self.exch
        self.remote(whole, whole, 0, self.re.at[0], self.partner()).wait_send()
        self.remote(whole, whole, 4, self.rb.at[0], self.partner()).wait_send()

        @pl.when(self.px < self.nx - 1)
        def _():
            self.remote(whole, whole, 1, self.rx.at[0], self.partner()).wait_send()

        @pl.when(self.pz < self.nz - 1)
        def _():
            self.remote(whole, whole, 2, self.ru.at[0], self.partner()).wait_send()

        @pl.when((self.pz > 0) & (self.px > 0))
        def _():
            self.remote(whole, whole, 3, self.rd.at[0], self.partner()).wait_send()


def kernel(
    sizes,
    q_hbm,
    k_hbm,
    v_hbm,
    g_hbm,
    gain_ref,
    dq_hbm,
    dk_hbm,
    dv_hbm,
    dgain_ref,
    *scratch,
):
    ny, nx, nz = sizes
    scratch = list(scratch)

    def take(n):
        out = scratch[:n]
        del scratch[:n]
        return out

    q, k, v, g = take(4)
    dq, dk, dv = take(3)
    scores, d_out, prior = take(3)
    out_loc, dk_loc, dv_loc = take(3)
    gtile, gin1, acc1, gin2, acc2, gin3, acc3, gin4 = take(8)
    bufs1, sems1 = take(10), take(6)
    bufs2, sems2 = take(10), take(6)
    in_sem, out_sem, gsend, g1r, g2r, g3r, g4r = take(7)

    y = lax.axis_index("dp")
    ctx = lax.axis_index("ctx")
    x = ctx // (2 * nz)
    z = (ctx // 2) % nz
    c = ctx % 2
    pos = (y, x, z, c)

    def device(y_, x_, z_, c_):
        return (y_, (x_ * nz + z_) * 2 + c_)

    loads = [pltpu.make_async_copy(src.at[0], dst, in_sem.at[i]) for i, (src, dst) in enumerate(((k_hbm, k), (v_hbm, v), (q_hbm, q), (g_hbm, g)))]
    for load in loads:
        load.start()

    def y_peer(i):
        return device((y + i) % ny, x, z, c)

    def x_peer(i):
        return device(y, (x + i) % nx, z, c)

    def z_peer(i):
        return device(y, x, (z + i) % nz, c)

    partner = device(y, x, z, 1 - c)
    barrier = pltpu.get_barrier_semaphore()
    pl.semaphore_signal(barrier, inc=1, device_id=partner, device_id_type=MESH)
    for count, peer in ((ny, y_peer), (nx, x_peer), (nz, z_peer)):
        for i in range(1, count):
            pl.semaphore_signal(barrier, inc=1, device_id=peer(i), device_id_type=MESH)

    one = Scan((nx, nz), pos, 1, bufs1, sems1)
    two = Scan((nx, nz), pos, -1, bufs2, sems2)
    one.clear()
    two.clear()

    def col(h):
        return pl.ds(pl.multiple_of(h * DIM, DIM), DIM)

    mine, other = c * HALF, (1 - c) * HALF

    def columns(ref, heads):
        return [ref[:, col(h)] for h in heads]

    def local_states(heads):
        ks, vs = columns(k, heads), columns(v, heads)
        states = [dot(kh, vh, 0, 0) for kh, vh in zip(ks, vs)]
        for h, state in zip(heads, states):
            one.own[pl.ds(h * CH, CH)] = state.reshape(CH, ROWS, DIM)

    loads[0].wait()
    loads[1].wait()

    for i in range(0, HALF, 4):
        local_states([other + i + u for u in range(4)])
        if i == 0:
            pl.semaphore_wait(barrier, ny + nx + nz - 2)
        for u in range(4):
            one.exch_copy(i + u).start()

    @pl.loop(0, HALF // 4)
    def _(i):
        local_states([mine + i * 4 + u for u in range(4)])

    loads[2].wait()
    loads[3].wait()

    keep = lax.broadcasted_iota(jnp.int32, (DIM, DIM), 0) >= lax.broadcasted_iota(jnp.int32, (DIM, DIM), 1)

    def before_one(heads):
        qs, ks, vs = columns(q, heads), columns(k, heads), columns(v, heads)
        raw = [dot(qh, kh, 1, 1) for qh, kh in zip(qs, ks)]
        lows = [jnp.where(keep, r, 0.0).astype(BF16) for r in raw]
        outs = [dot(low, vh, 1, 0) for low, vh in zip(lows, vs)]
        for h, low, out in zip(heads, lows, outs):
            scores[h] = low
            out_loc[h] = out

    def pass_one(heads, states):
        qs = columns(q, heads)
        gfs = [gh.astype(F32) for gh in columns(g, heads)]
        gains = columns(gain_ref, heads)
        locs = [out_loc[h] for h in heads]
        lows = [state.astype(BF16) for state in states]
        outs = [loc + dot(qh, low, 1, 0) for loc, qh, low in zip(locs, qs, lows)]
        invs = [lax.rsqrt(jnp.mean(out * out, axis=1, keepdims=True) + EPSILON) for out in outs]
        normeds = [out * inv for out, inv in zip(outs, invs)]
        gns = [gf * gain for gf, gain in zip(gfs, gains)]
        means = [jnp.mean(gn * normed, axis=1, keepdims=True) for gn, normed in zip(gns, normeds)]
        ds = [((gn - normed * mean) * inv).astype(BF16) for gn, normed, mean, inv in zip(gns, normeds, means, invs)]
        grads = [dot(qh, d, 0, 0) for qh, d in zip(qs, ds)]
        terms = [jnp.sum((gf * normed).reshape(DIM // 8, 8, DIM), axis=0) for gf, normed in zip(gfs, normeds)]
        for h, low, d, grad, term in zip(heads, lows, ds, grads, terms):
            prior[h] = low
            d_out[h] = d
            two.own[pl.ds(h * CH, CH)] = grad.reshape(CH, ROWS, DIM)
            gtile[h] = term

    def between(heads):
        ds, lows, scs = [d_out[h] for h in heads], [prior[h] for h in heads], [scores[h] for h in heads]
        qs, ks, vs = columns(q, heads), columns(k, heads), columns(v, heads)
        raw = [dot(d, vh, 1, 1) for d, vh in zip(ds, vs)]
        dvs = [dot(sc, d, 0, 0) for sc, d in zip(scs, ds)]
        pqs = [dot(d, low, 1, 1) for d, low in zip(ds, lows)]
        gss = [jnp.where(keep, r, 0.0).astype(BF16) for r in raw]
        dqs = [(dot(gs, kh, 1, 0) + pq).astype(BF16) for gs, kh, pq in zip(gss, ks, pqs)]
        dks = [dot(gs, qh, 0, 0) for gs, qh in zip(gss, qs)]
        for h, dqh, dkh, dvh in zip(heads, dqs, dks, dvs):
            dq[:, col(h)] = dqh
            dk_loc[h] = dkh
            dv_loc[h] = dvh

    def store(ref, hbm, i, h):
        return pltpu.make_async_copy(ref.at[:, col(h)], hbm.at[0, :, col(h)], out_sem.at[i])

    def pass_two(heads, states):
        ks, vs = columns(k, heads), columns(v, heads)
        dks, dvs = [dk_loc[h] for h in heads], [dv_loc[h] for h in heads]
        lows = [state.astype(BF16) for state in states]
        dks = [(part + dot(vh, low, 1, 1)).astype(BF16) for part, vh, low in zip(dks, vs, lows)]
        dvs = [(part + dot(kh, low, 1, 0)).astype(BF16) for part, kh, low in zip(dvs, ks, lows)]
        for h, dkh, dvh in zip(heads, dks, dvs):
            dk[:, col(h)] = dkh
            dv[:, col(h)] = dvh
        for h in heads:
            store(dk, dk_hbm, 1, h).start()
            store(dv, dv_hbm, 2, h).start()

    ry, rx = HEADS // ny, HEADS // ny // nx

    def g1_copy(i):
        src = gtile.at[pl.ds(((y + i) % ny) * ry, ry)]
        return pltpu.make_async_remote_copy(
            src_ref=src, dst_ref=gin1.at[i - 1], send_sem=gsend.at[0], recv_sem=g1r.at[i - 1], device_id=y_peer(i), device_id_type=MESH
        )

    def g2_copy(i):
        src = acc1.at[pl.ds(((x + i) % nx) * rx, rx)]
        return pltpu.make_async_remote_copy(
            src_ref=src, dst_ref=gin2.at[i - 1], send_sem=gsend.at[1], recv_sem=g2r.at[i - 1], device_id=x_peer(i), device_id_type=MESH
        )

    def g3_copy(i):
        return pltpu.make_async_remote_copy(
            src_ref=acc2, dst_ref=gin3.at[i - 1], send_sem=gsend.at[2], recv_sem=g3r.at[i - 1], device_id=z_peer(i), device_id_type=MESH
        )

    def g4_copy():
        return pltpu.make_async_remote_copy(
            src_ref=acc3, dst_ref=gin4, send_sem=gsend.at[3], recv_sem=g4r, device_id=partner, device_id_type=MESH
        )

    def gain_step(stage):
        if stage == 0:
            for i in range(1, ny):
                g1_copy(i).start()
        elif stage == 1:
            total = gtile[pl.ds(y * ry, ry)]
            for i in range(1, ny):
                g1_copy(i).wait_recv()
                total = total + gin1[i - 1]
            acc1[...] = total
            for i in range(1, nx):
                g2_copy(i).start()
        elif stage == 2:
            total = acc1[pl.ds(x * rx, rx)]
            for i in range(1, nx):
                g2_copy(i).wait_recv()
                total = total + gin2[i - 1]
            acc2[...] = total
            for i in range(1, nz):
                g3_copy(i).start()
        elif stage == 3:
            total = acc2[...]
            for i in range(1, nz):
                g3_copy(i).wait_recv()
                total = total + gin3[i - 1]
            acc3[...] = total
            g4_copy().start()
        else:
            g4_copy().wait_recv()
            scale = 1.0 / math.sqrt(ny * nx * nz * 2 * DIM)
            dgain_ref[...] = jnp.sum(acc3[...] + gin4[...], axis=1) * scale

    span = HOP * (nz - 1)
    row1 = HOP * x + span + CH - 1
    begin2 = HOP * (nx - 1) + span + CH - 1 + CH * LAG + HOP
    row2 = begin2 + HOP * (nx - 1 - x) + span + CH - 1
    gain_begin = HOP * (nx - 1) + span + CHUNKS + CH * LAG
    steps = begin2 + HOP * (nx - 1) + span + CHUNKS + CH * LAG

    def finishing(first, s, scan, work, after):
        f = s - first
        m = f // CH

        @pl.when((f >= 0) & (f % CH == 0) & (m < LAG))
        def _():
            work([mine + m], [scan.finish(m)])

        @pl.when((f % CH == 0) & (m >= LAG) & (m < HALF))
        def _():
            state = scan.finish(m)
            work([mine + m, other + m - LAG], [state, scan.finished(m - LAG)])
            after(m - LAG)

        @pl.when((f % CH == 0) & (m >= HALF) & (m < HALF + LAG))
        def _():
            work([other + m - LAG], [scan.finished(m - LAG)])
            after(m - LAG)

    def swap_two(m):
        two.exch_copy(m).start()

    def nothing(m):
        pass

    @pl.loop(0, steps)
    def _(s):
        one.forward(s)
        two.forward(s - begin2)
        finishing(row1, s, one, pass_one, swap_two)
        finishing(row2, s, two, pass_two, nothing)

        @pl.when((s < CHUNKS) & (s % CH == 0))
        def _():
            m = s // CH
            before_one([mine + m, other + m])

        mid = s - (row1 + CHUNKS + CH * LAG)

        @pl.when((mid >= 0) & (mid < CHUNKS) & (mid % CH == 0))
        def _():
            m = mid // CH
            between([mine + m, other + m])

        @pl.when(mid == CHUNKS)
        def _():
            pltpu.make_async_copy(dq, dq_hbm.at[0], out_sem.at[0]).start()

        for stage in range(5):

            @pl.when(s == gain_begin + 4 * stage)
            def _(stage=stage):
                gain_step(stage)

    one.drain()
    two.drain()
    for i in range(1, ny):
        g1_copy(i).wait_send()
    for i in range(1, nx):
        g2_copy(i).wait_send()
    for i in range(1, nz):
        g3_copy(i).wait_send()
    g4_copy().wait_send()
    for i, (ref, hbm) in enumerate(((dq, dq_hbm), (dk, dk_hbm), (dv, dv_hbm))):
        pltpu.make_async_copy(ref, hbm.at[0], out_sem.at[i]).wait()


def build(mesh, nx, nz):
    ny = mesh.shape["dp"]
    width = HEADS * DIM
    ry, rx = HEADS // ny, HEADS // ny // nx

    def scan_scratch():
        state = pltpu.VMEM((CHUNKS, ROWS, DIM), F32)
        return [
            pltpu.VMEM((2 * CHUNKS, ROWS, DIM), F32),
            *[state] * 9,
            pltpu.SemaphoreType.DMA((HALF,)),
            *[pltpu.SemaphoreType.DMA((CHUNKS,))] * 3,
            pltpu.SemaphoreType.DMA((HALF,)),
            pltpu.SemaphoreType.DMA((5,)),
        ]

    scratch = [
        *[pltpu.VMEM((DIM, width), BF16)] * 7,
        *[pltpu.VMEM((HEADS, DIM, DIM), BF16)] * 3,
        *[pltpu.VMEM((HEADS, DIM, DIM), F32)] * 3,
        pltpu.VMEM((HEADS, 8, DIM), F32),
        pltpu.VMEM((ny - 1, ry, 8, DIM), F32),
        pltpu.VMEM((ry, 8, DIM), F32),
        pltpu.VMEM((nx - 1, rx, 8, DIM), F32),
        pltpu.VMEM((rx, 8, DIM), F32),
        pltpu.VMEM((nz - 1, rx, 8, DIM), F32),
        pltpu.VMEM((rx, 8, DIM), F32),
        pltpu.VMEM((rx, 8, DIM), F32),
        *scan_scratch(),
        *scan_scratch(),
        pltpu.SemaphoreType.DMA((4,)),
        pltpu.SemaphoreType.DMA((3,)),
        pltpu.SemaphoreType.DMA((4,)),
        pltpu.SemaphoreType.DMA((ny - 1,)),
        pltpu.SemaphoreType.DMA((nx - 1,)),
        pltpu.SemaphoreType.DMA((nz - 1,)),
        pltpu.SemaphoreType.DMA,
    ]

    def body(queries, key_rows, value_rows, out_grad, norm_gain):
        rows = jax.ShapeDtypeStruct(queries.shape, BF16)
        dq, dk, dv, dgain = pl.pallas_call(
            functools.partial(kernel, (ny, nx, nz)),
            out_shape=(rows, rows, rows, jax.ShapeDtypeStruct((rx, DIM), F32)),
            in_specs=[pl.BlockSpec(memory_space=pl.ANY)] * 4 + [pl.BlockSpec(memory_space=pltpu.VMEM)],
            out_specs=[pl.BlockSpec(memory_space=pl.ANY)] * 3 + [pl.BlockSpec(memory_space=pltpu.VMEM)],
            scratch_shapes=scratch,
            compiler_params=pltpu.CompilerParams(
                collective_id=0, has_side_effects=True, vmem_limit_bytes=62 * 1024 * 1024
            ),
        )(queries, key_rows, value_rows, out_grad, norm_gain.reshape(1, width))
        share = rx * DIM // (2 * nz)
        place = lax.rem(lax.axis_index("ctx"), 2 * nz) * share
        return dq, dk, dv, lax.dynamic_slice(dgain.reshape(rx * DIM), (place,), (share,))

    placed = P("dp", "ctx", None)
    return jax.shard_map(
        body,
        mesh=mesh,
        in_specs=(placed, placed, placed, placed, P()),
        out_specs=(placed, placed, placed, P(("dp", "ctx"))),
        check_vma=False,
    )


def solution(mesh):
    return build(mesh, 4, 8)
```

time: 762 us -> 106 us (0.14)
  waiting for transfers between devices: 382 us -> 0 us
  other arithmetic: 203 us -> 0 us
  Pallas kernels: 0 us -> 100 us
  blocking collectives: 76.6 us -> 0 us
  local copies, waits for them, and re-layouts: 57.2 us -> 5.11 us
  matrix products: 19 us -> 0 us
  between operations: 14.2 us -> 0.66 us
    all_gather x2 -> x0, waiting for transfers between devices: 382 us -> none  [entering(): pieces = lax.all_gather(value, axis)]
    select_n x126 -> x0, other arithmetic: 200 us -> none  [lap(): return jnp.where(position < mine, longer, running)]
    pallas_call x0 -> x1, Pallas kernels: none -> 100 us  [body(): pl.pallas_call(functools.partial(kernel, (ny, nx, nz)), out_shape=(rows,...]
    unnamed x1 -> x0, blocking collectives: 76.6 us -> none
    rev x1 -> x0, local copies, waits for them, and re-layouts: 44.9 us -> none  [entering(): pieces = pieces[::-1]]
    dot_general x12 -> x0, matrix products: 19 us -> none  [the longest x2 3.09 us: masked_scores(): jnp.einsum('lhe,mhe->hlm', left_rows, right_rows, preferred_element_type=...]
  transfers between devices with their start and end apart: 2 -> 0, of which waited for: 2 -> 0; matrix products, arithmetic and copies ran while one was open for 2% -> 0% of each run, Pallas kernels for 0% -> 0%
where the time goes in v1:
time: 106 us
  Pallas kernels  100 us (94%)
  local copies, waits for them, and re-layouts  5.11 us (5%)
    pallas_call x1, Pallas kernels, body(): pl.pallas_call(functools.partial(kernel, (ny, nx, nz)), out_shape=(rows,...  100 us
    unnamed x9, local copies, waits for them, and re-layouts  4.53 us

profile of v1, /device:TPU:1, one launch (start us, length us, event | category | flops | bytes accessed | tf_op | source)
XLA Modules:
  0.0 106.1 jit_solution(14136934843310527312)
XLA Ops:
  0.6 100.4 %shard_map.84 = (bf16[1,128,2048]{2,1,0:T(8,128)(2,1)}, bf16[1,128,2048]{2,1,0:T(8,128)(2,1)}, bf16[1,128,2048]{2,1,0:T(8,128)(2,1)}, f32[1,128]{1,0:T(1,128)}) custom-call(bf16[1,128,2048]{2,1,0:T(8,128)(2,1)} %q_hbm.1, bf16[1,128,2048]{2,1,0:T(8,128)(2,1)} %k_hbm.1, bf16[1,128,2048]{2,1,0:T(8,128)(2,1)} %v_hbm.1, bf16[1,128,2048]{2,1,0:T(8,128)(2,1)} %g_hbm.1, ...), custom_call_target="tpu_custom_call" | custom-call | tf_op jit(solution)/shard_map/pallas_call | solution.py:504
  101.0 0.0 copy-start.2
  101.0 0.6 copy-done.2
  101.6 0.6 dynamic-slice_bitcast_fusion
  102.2 0.0 copy-start.1
  102.2 1.9 %copy.12 = bf16[1,128,2048]{2,1,0:T(8,128)(2,1)} copy(bf16[1,128,2048]{2,1,0:T(8,128)(2,1)} %get-tuple-element.16) | data formatting | bytes 1048576
  104.1 0.0 copy-done.1
  104.1 0.0 copy-start
  104.1 0.8 copy.13
  104.9 0.4 copy-done
  105.3 0.8 copy.14
Async XLA Ops:
  101.0 0.6 copy-start.2
  102.2 1.9 %copy-start.1 = (bf16[1,128,2048]{2,1,0:T(8,128)(2,1)S(1)}, bf16[1,128,2048]{2,1,0:T(8,128)(2,1)}, u32[]{:S(2)}) copy-start(bf16[1,128,2048]{2,1,0:T(8,128)(2,1)} %get-tuple-element.17) | copy-start | bytes 1572868
  104.1 1.2 %copy-start = (bf16[1,128,2048]{2,1,0:T(8,128)(2,1)S(1)}, bf16[1,128,2048]{2,1,0:T(8,128)(2,1)}, u32[]{:S(2)}) copy-start(bf16[1,128,2048]{2,1,0:T(8,128)(2,1)} %get-tuple-element.18) | copy-start | bytes 1572868

commit v2 on v1

--- a/solution.py
+++ b/solution.py
@@ -17,7 +17,7 @@
 BF16 = jnp.bfloat16
 
 CH = 2
-HOP = 3
+HOP = 2
 LAG = 2
 ROWS = DIM // CH
 CHUNKS = HALF * CH
@@ -460,6 +460,14 @@
         pltpu.make_async_copy(ref, hbm.at[0], out_sem.at[i]).wait()
 
 
+def hand_over(a, b, c, a_out, b_out, c_out, sems):
+    copies = [pltpu.make_async_copy(src, dst, sems.at[i]) for i, (src, dst) in enumerate(((a, a_out), (b, b_out), (c, c_out)))]
+    for copy in copies:
+        copy.start()
+    for copy in copies:
+        copy.wait()
+
+
 def build(mesh, nx, nz):
     ny = mesh.shape["dp"]
     width = HEADS * DIM
@@ -511,6 +519,14 @@
                 collective_id=0, has_side_effects=True, vmem_limit_bytes=62 * 1024 * 1024
             ),
         )(queries, key_rows, value_rows, out_grad, norm_gain.reshape(1, width))
+        dq, dk, dv = pl.pallas_call(
+            hand_over,
+            out_shape=(rows, rows, rows),
+            in_specs=[pl.BlockSpec(memory_space=pl.ANY)] * 3,
+            out_specs=[pl.BlockSpec(memory_space=pl.ANY)] * 3,
+            scratch_shapes=[pltpu.SemaphoreType.DMA((3,))],
+            compiler_params=pltpu.CompilerParams(vmem_limit_bytes=62 * 1024 * 1024),
+        )(dq, dk, dv)
         share = rx * DIM // (2 * nz)
         place = lax.rem(lax.axis_index("ctx"), 2 * nz) * share
         return dq, dk, dv, lax.dynamic_slice(dgain.reshape(rx * DIM), (place,), (share,))

time: 106 us -> 160 us (1.51)
  Pallas kernels: 100 us -> 158 us
  local copies, waits for them, and re-layouts: 5.11 us -> 1.24 us
    pallas_call x0 -> x1, Pallas kernels: none -> 48.8 us  [body(): pl.pallas_call(hand_over, out_shape=(rows, rows, rows), in_specs=[pl.Bloc...]
    pallas_call x1, Pallas kernels: 100 us -> 109 us  [body(): pl.pallas_call(functools.partial(kernel, (ny, nx, nz)), out_shape=(rows,...]
    unnamed x9 -> x2, local copies, waits for them, and re-layouts: 4.53 us -> 0.66 us
where the time goes in v2:
time: 160 us
  Pallas kernels  158 us (99%)
    pallas_call x1, Pallas kernels, body(): pl.pallas_call(functools.partial(kernel, (ny, nx, nz)), out_shape=(rows,...  109 us
    pallas_call x1, Pallas kernels, body(): pl.pallas_call(hand_over, out_shape=(rows, rows, rows), in_specs=[pl.Bloc...  48.8 us

profile of v2, /device:TPU:1, one launch (start us, length us, event | category | flops | bytes accessed | tf_op | source)
XLA Modules:
  0.0 159.9 jit_solution(6628566329326020953)
XLA Ops:
  0.6 109.3 %shard_map.84 = (bf16[1,128,2048]{2,1,0:T(8,128)(2,1)}, bf16[1,128,2048]{2,1,0:T(8,128)(2,1)}, bf16[1,128,2048]{2,1,0:T(8,128)(2,1)}, f32[1,128]{1,0:T(1,128)}) custom-call(bf16[1,128,2048]{2,1,0:T(8,128)(2,1)} %q_hbm.1, bf16[1,128,2048]{2,1,0:T(8,128)(2,1)} %k_hbm.1, bf16[1,128,2048]{2,1,0:T(8,128)(2,1)} %v_hbm.1, bf16[1,128,2048]{2,1,0:T(8,128)(2,1)} %g_hbm.1, ...), custom_call_target="tpu_custom_call" | custom-call | tf_op jit(solution)/shard_map/pallas_call | solution.py:512
  109.9 0.0 copy-start
  109.9 0.7 copy-done
  110.6 0.6 dynamic-slice_bitcast_fusion
  111.2 48.8 %shard_map.85 = (bf16[1,128,2048]{2,1,0:T(8,128)(2,1)}, bf16[1,128,2048]{2,1,0:T(8,128)(2,1)}, bf16[1,128,2048]{2,1,0:T(8,128)(2,1)}) custom-call(bf16[1,128,2048]{2,1,0:T(8,128)(2,1)} %get-tuple-element.11.a, bf16[1,128,2048]{2,1,0:T(8,128)(2,1)} %get-tuple-element.12.b, bf16[1,128,2048]{2,1,0:T(8,128)(2,1)} %get-tuple-element.13.c), custom_call_target="tpu_custom_call" | custom-call | tf_op jit(solution)/shard_map/pallas_call | solution.py:522
Async XLA Ops:
  109.9 0.7 copy-start

commit v3 on v2

--- a/solution.py
+++ b/solution.py
@@ -16,15 +16,16 @@
 F32 = jnp.float32
 BF16 = jnp.bfloat16
 
-CH = 2
-HOP = 2
 LAG = 2
-ROWS = DIM // CH
-CHUNKS = HALF * CH
+SUM_LAG = 2
 
 
 def dot(a, b, ca, cb):
     return lax.dot_general(a, b, (((ca,), (cb,)), ((), ())), preferred_element_type=F32)
+
+
+def turn(e):
+    return 4 - e // 2 + (e % 2) * (e // 2 + (e + 1) // 2)
 
 
 class Scan:
@@ -33,11 +34,11 @@
         self.y, self.x, self.z, self.c = pos
         self.order = order
         if order > 0:
-            self.px, self.pz, self.pc = self.x, self.z, self.c
+            self.px, self.pc = self.x, self.c
         else:
-            self.px, self.pz, self.pc = self.nx - 1 - self.x, self.nz - 1 - self.z, 1 - self.c
-        (self.own, self.exch, self.xin, self.a, self.upin, self.upout, self.dnin, self.dnout, self.bkin, self.bkout) = bufs
-        self.re, self.rx, self.ru, self.rd, self.rb, self.sends = sems
+            self.px, self.pc = self.nx - 1 - self.x, 1 - self.c
+        self.own, self.exch, self.s, self.gin, self.r, self.rin, self.pout, self.pin, self.bkin, self.bkout = bufs
+        self.re, self.ri, self.rx, self.ro, self.rb, self.sends = sems
 
     def device(self, x, z, c):
         return (self.y, (x * self.nz + z) * 2 + c)
@@ -51,126 +52,93 @@
         )
 
     def exch_copy(self, m):
-        src = self.own.at[pl.ds(((1 - self.c) * HALF + m) * CH, CH)]
-        return self.remote(src, self.exch.at[pl.ds(m * CH, CH)], 0, self.re.at[m], self.partner())
-
-    def x_copy(self, j):
-        return self.remote(
-            self.a.at[j], self.xin.at[j], 1, self.rx.at[j], self.device(self.x + self.order, self.z, self.c)
-        )
-
-    def up_copy(self, src, j):
-        return self.remote(
-            src.at[j], self.upin.at[j], 2, self.ru.at[j], self.device(self.x, self.z + self.order, self.c)
-        )
-
-    def dn_copy(self, src, j):
-        return self.remote(
-            src.at[j], self.dnin.at[j], 3, self.rd.at[j], self.device(self.x, self.z - self.order, self.c)
-        )
+        return self.remote(self.own.at[(1 - self.c) * HALF + m], self.exch.at[m], 0, self.re.at[m], self.partner())
+
+    def in_copy(self, m, slot):
+        return self.remote(self.s.at[m], self.gin.at[slot], 1, self.ri.at[slot], self.device(self.x, m, self.c))
+
+    def out_copy(self, m, slot):
+        return self.remote(self.pout.at[m], self.pin.at[slot], 2, self.ro.at[slot], self.device(self.x, m, self.c))
 
     def bk_copy(self, m):
-        part = pl.ds(m * CH, CH)
-        return self.remote(self.bkout.at[part], self.bkin.at[part], 4, self.rb.at[m], self.partner())
-
-    def clear(self):
-        @pl.when(self.px == 0)
+        return self.remote(self.bkout.at[m], self.bkin.at[m], 3, self.rb.at[m], self.partner())
+
+    def x_copy(self, i):
+        to = self.device(self.x + i * self.order, self.z, self.c)
+        return self.remote(self.r, self.rin.at[i - 1], 3 + i, self.rx.at[i - 1], to)
+
+    def add_chip(self, m):
+        self.exch_copy(m).wait_recv()
+        total = self.own[self.c * HALF + m] + self.exch[m]
+
+        @pl.when(m == self.z)
         def _():
-            self.xin[...] = jnp.zeros(self.xin.shape, F32)
-
-        @pl.when(self.pz == 0)
+            self.gin[m] = total
+
+        @pl.when(m != self.z)
         def _():
-            self.upin[...] = jnp.zeros(self.upin.shape, F32)
-
-        @pl.when((self.px == 0) | (self.pz == self.nz - 1))
+            self.s[m] = total
+            self.in_copy(m, self.z).start()
+
+    def add_row(self):
+        for e in range(self.nz - 1):
+            source = (self.z + self.nz - turn(e)) % self.nz
+            self.in_copy(source, source).wait_recv()
+        total = self.gin[0]
+        for m in range(1, self.nz):
+            total = total + self.gin[m]
+        self.r[...] = total
+        for i in range(1, self.nx):
+
+            @pl.when(self.px + i < self.nx)
+            def _(i=i):
+                self.x_copy(i).start()
+
+    def spread(self):
+        self.pout[0] = jnp.zeros((DIM, DIM), F32)
+        for i in range(1, self.nx):
+
+            @pl.when(self.px >= i)
+            def _(i=i):
+                self.x_copy(i).wait_recv()
+                self.pout[0] = self.pout[0] + self.rin[i - 1]
+
+        total = self.pout[0]
+        for m in range(self.nz):
+            place = m if self.order > 0 else self.nz - 1 - m
+            self.pout[place] = total
+            total = total + self.gin[place]
+        self.pin[self.z] = self.pout[self.z]
+
+        @pl.loop(0, self.nz - 1)
+        def _(e):
+            self.out_copy((self.z + turn(e)) % self.nz, self.z).start()
+
+    def finish(self, m):
+        @pl.when(m != self.z)
         def _():
-            self.dnin[...] = jnp.zeros(self.dnin.shape, F32)
-
-    def along_x(self, j):
-        @pl.when(j % CH == 0)
-        def _():
-            self.exch_copy(j // CH).wait_recv()
-
-        @pl.when(self.px > 0)
-        def _():
-            self.x_copy(j).wait_recv()
-
-        self.a[j] = self.own[self.c * CHUNKS + j] + self.exch[j] + self.xin[j]
-
-        @pl.when(self.px < self.nx - 1)
-        def _():
-            self.x_copy(j).start()
-
-        @pl.when(self.pz == 0)
-        def _():
-            self.up_copy(self.a, j).start()
-
-        @pl.when((self.pz == self.nz - 1) & (self.px > 0))
-        def _():
-            self.dn_copy(self.xin, j).start()
-
-    def up(self, j):
-        self.up_copy(self.upout, j).wait_recv()
-
-        @pl.when(self.pz < self.nz - 1)
-        def _():
-            self.upout[j] = self.upin[j] + self.a[j]
-            self.up_copy(self.upout, j).start()
-
-    def down(self, j):
-        self.dn_copy(self.dnout, j).wait_recv()
-
-        @pl.when(self.pz > 0)
-        def _():
-            self.dnout[j] = self.dnin[j] + self.xin[j]
-            self.dn_copy(self.dnout, j).start()
-
-    def forward(self, t):
-        jx = t - HOP * self.px
-        ju = jx - HOP * self.pz
-        jd = jx - HOP * (self.nz - 1 - self.pz)
-
-        @pl.when((jx >= 0) & (jx < CHUNKS))
-        def _():
-            self.along_x(jx)
-
-        @pl.when((ju >= 0) & (ju < CHUNKS) & (self.pz > 0))
-        def _():
-            self.up(ju)
-
-        @pl.when((jd >= 0) & (jd < CHUNKS) & (self.pz < self.nz - 1) & (self.px > 0))
-        def _():
-            self.down(jd)
-
-    def finish(self, m):
-        part = pl.ds(m * CH, CH)
-        before = (self.upin[part] + self.xin[part] + self.dnin[part]).reshape(DIM, DIM)
-        first = self.own[pl.ds(self.c * CHUNKS + m * CH, CH)].reshape(DIM, DIM)
-        second = self.exch[part].reshape(DIM, DIM)
-        self.bkout[part] = jnp.where(self.pc == 0, before + first, before).reshape(CH, ROWS, DIM)
+            self.out_copy(m, m).wait_recv()
+
+        before = self.pin[m]
+        self.bkout[m] = jnp.where(self.pc == 0, before + self.own[self.c * HALF + m], before)
         self.bk_copy(m).start()
-        return jnp.where(self.pc == 1, before + second, before)
+        return jnp.where(self.pc == 1, before + self.exch[m], before)
 
     def finished(self, m):
         self.bk_copy(m).wait_recv()
-        return self.bkin[pl.ds(m * CH, CH)].reshape(DIM, DIM)
+        return self.bkin[m]
 
     def drain(self):
-        whole = self.exch
-        self.remote(whole, whole, 0, self.re.at[0], self.partner()).wait_send()
-        self.remote(whole, whole, 4, self.rb.at[0], self.partner()).wait_send()
-
-        @pl.when(self.px < self.nx - 1)
-        def _():
-            self.remote(whole, whole, 1, self.rx.at[0], self.partner()).wait_send()
-
-        @pl.when(self.pz < self.nz - 1)
-        def _():
-            self.remote(whole, whole, 2, self.ru.at[0], self.partner()).wait_send()
-
-        @pl.when((self.pz > 0) & (self.px > 0))
-        def _():
-            self.remote(whole, whole, 3, self.rd.at[0], self.partner()).wait_send()
+        some = pl.ds(0, self.nz - 1)
+        self.remote(self.exch, self.exch, 0, self.re.at[0], self.partner()).wait_send()
+        self.remote(self.s.at[some], self.gin.at[some], 1, self.ri.at[0], self.partner()).wait_send()
+        self.remote(self.pout.at[some], self.pin.at[some], 2, self.ro.at[0], self.partner()).wait_send()
+        self.remote(self.bkout, self.bkin, 3, self.rb.at[0], self.partner()).wait_send()
+        for i in range(1, self.nx):
+
+            @pl.when(self.px + i < self.nx)
+            def _(i=i):
+                self.x_copy(i).wait_send()
 
 
 def kernel(
@@ -235,8 +203,6 @@
 
     one = Scan((nx, nz), pos, 1, bufs1, sems1)
     two = Scan((nx, nz), pos, -1, bufs2, sems2)
-    one.clear()
-    two.clear()
 
     def col(h):
         return pl.ds(pl.multiple_of(h * DIM, DIM), DIM)
@@ -250,21 +216,25 @@
         ks, vs = columns(k, heads), columns(v, heads)
         states = [dot(kh, vh, 0, 0) for kh, vh in zip(ks, vs)]
         for h, state in zip(heads, states):
-            one.own[pl.ds(h * CH, CH)] = state.reshape(CH, ROWS, DIM)
+            one.own[h] = state
 
     loads[0].wait()
     loads[1].wait()
 
+    def place(e):
+        return (z + turn(e)) % nz
+
     for i in range(0, HALF, 4):
-        local_states([other + i + u for u in range(4)])
+        local_states([other + place(i + u) for u in range(4)])
         if i == 0:
             pl.semaphore_wait(barrier, ny + nx + nz - 2)
         for u in range(4):
-            one.exch_copy(i + u).start()
-
-    @pl.loop(0, HALF // 4)
-    def _(i):
-        local_states([mine + i * 4 + u for u in range(4)])
+            one.exch_copy(place(i + u)).start()
+
+    for i in range(0, HALF, 4):
+        local_states([mine + place(i + u) for u in range(4)])
+        for u in range(4):
+            one.add_chip(place(i + u))
 
     loads[2].wait()
     loads[3].wait()
@@ -297,7 +267,7 @@
         for h, low, d, grad, term in zip(heads, lows, ds, grads, terms):
             prior[h] = low
             d_out[h] = d
-            two.own[pl.ds(h * CH, CH)] = grad.reshape(CH, ROWS, DIM)
+            two.own[h] = grad
             gtile[h] = term
 
     def between(heads):
@@ -386,66 +356,61 @@
             scale = 1.0 / math.sqrt(ny * nx * nz * 2 * DIM)
             dgain_ref[...] = jnp.sum(acc3[...] + gin4[...], axis=1) * scale
 
-    span = HOP * (nz - 1)
-    row1 = HOP * x + span + CH - 1
-    begin2 = HOP * (nx - 1) + span + CH - 1 + CH * LAG + HOP
-    row2 = begin2 + HOP * (nx - 1 - x) + span + CH - 1
-    gain_begin = HOP * (nx - 1) + span + CHUNKS + CH * LAG
-    steps = begin2 + HOP * (nx - 1) + span + CHUNKS + CH * LAG
-
-    def finishing(first, s, scan, work, after):
-        f = s - first
-        m = f // CH
-
-        @pl.when((f >= 0) & (f % CH == 0) & (m < LAG))
-        def _():
-            work([mine + m], [scan.finish(m)])
-
-        @pl.when((f % CH == 0) & (m >= LAG) & (m < HALF))
-        def _():
-            state = scan.finish(m)
-            work([mine + m, other + m - LAG], [state, scan.finished(m - LAG)])
-            after(m - LAG)
-
-        @pl.when((f % CH == 0) & (m >= HALF) & (m < HALF + LAG))
-        def _():
-            work([other + m - LAG], [scan.finished(m - LAG)])
-            after(m - LAG)
-
-    def swap_two(m):
-        two.exch_copy(m).start()
+    def arrival(e):
+        return (z + nz - turn((e + nz - 1) % nz)) % nz
+
+    def finishing(scan, work, after, last):
+        @pl.loop(0, HALF + LAG + SUM_LAG)
+        def _(e):
+            @pl.when(e >= LAG + SUM_LAG)
+            def _():
+                last(arrival(e - LAG - SUM_LAG))
+
+            @pl.when(e < LAG)
+            def _():
+                m = arrival(e)
+                work([mine + m], [scan.finish(m)])
+
+            @pl.when((e >= LAG) & (e < HALF))
+            def _():
+                m, n = arrival(e), arrival(e - LAG)
+                state = scan.finish(m)
+                work([mine + m, other + n], [state, scan.finished(n)])
+                after(n)
+
+            @pl.when((e >= HALF) & (e < HALF + LAG))
+            def _():
+                n = arrival(e - LAG)
+                work([other + n], [scan.finished(n)])
+                after(n)
 
     def nothing(m):
         pass
 
-    @pl.loop(0, steps)
-    def _(s):
-        one.forward(s)
-        two.forward(s - begin2)
-        finishing(row1, s, one, pass_one, swap_two)
-        finishing(row2, s, two, pass_two, nothing)
-
-        @pl.when((s < CHUNKS) & (s % CH == 0))
+    @pl.loop(0, HALF)
+    def _(m):
+        before_one([mine + m, other + m])
+
+    one.add_row()
+    one.spread()
+    finishing(one, pass_one, lambda m: two.exch_copy(m).start(), two.add_chip)
+    gain_step(0)
+
+    @pl.loop(0, HALF)
+    def _(m):
+        between([mine + m, other + m])
+
+        @pl.when(m == HALF // 2)
         def _():
-            m = s // CH
-            before_one([mine + m, other + m])
-
-        mid = s - (row1 + CHUNKS + CH * LAG)
-
-        @pl.when((mid >= 0) & (mid < CHUNKS) & (mid % CH == 0))
-        def _():
-            m = mid // CH
-            between([mine + m, other + m])
-
-        @pl.when(mid == CHUNKS)
-        def _():
-            pltpu.make_async_copy(dq, dq_hbm.at[0], out_sem.at[0]).start()
-
-        for stage in range(5):
-
-            @pl.when(s == gain_begin + 4 * stage)
-            def _(stage=stage):
-                gain_step(stage)
+            gain_step(1)
+
+    pltpu.make_async_copy(dq, dq_hbm.at[0], out_sem.at[0]).start()
+    gain_step(2)
+    two.add_row()
+    two.spread()
+    gain_step(3)
+    finishing(two, pass_two, nothing, nothing)
+    gain_step(4)
 
     one.drain()
     two.drain()
@@ -460,12 +425,17 @@
         pltpu.make_async_copy(ref, hbm.at[0], out_sem.at[i]).wait()
 
 
-def hand_over(a, b, c, a_out, b_out, c_out, sems):
-    copies = [pltpu.make_async_copy(src, dst, sems.at[i]) for i, (src, dst) in enumerate(((a, a_out), (b, b_out), (c, c_out)))]
-    for copy in copies:
-        copy.start()
-    for copy in copies:
-        copy.wait()
+def hand_over(a, b, c, a_out, b_out, c_out, a_buf, b_buf, c_buf, sems):
+    trips = ((a, a_buf, a_out), (b, b_buf, b_out), (c, c_buf, c_out))
+    loads = [pltpu.make_async_copy(src.at[0], buf, sems.at[0, i]) for i, (src, buf, _) in enumerate(trips)]
+    stores = [pltpu.make_async_copy(buf, dst.at[0], sems.at[1, i]) for i, (_, buf, dst) in enumerate(trips)]
+    for load in loads:
+        load.start()
+    for load, store in zip(loads, stores):
+        load.wait()
+        store.start()
+    for store in stores:
+        store.wait()
 
 
 def build(mesh, nx, nz):
@@ -474,14 +444,17 @@
     ry, rx = HEADS // ny, HEADS // ny // nx
 
     def scan_scratch():
-        state = pltpu.VMEM((CHUNKS, ROWS, DIM), F32)
+        state = pltpu.VMEM((HALF, DIM, DIM), F32)
         return [
-            pltpu.VMEM((2 * CHUNKS, ROWS, DIM), F32),
-            *[state] * 9,
-            pltpu.SemaphoreType.DMA((HALF,)),
-            *[pltpu.SemaphoreType.DMA((CHUNKS,))] * 3,
-            pltpu.SemaphoreType.DMA((HALF,)),
-            pltpu.SemaphoreType.DMA((5,)),
+            pltpu.VMEM((HEADS, DIM, DIM), F32),
+            *[state] * 3,
+            pltpu.VMEM((DIM, DIM), F32),
+            pltpu.VMEM((nx - 1, DIM, DIM), F32),
+            *[state] * 4,
+            *[pltpu.SemaphoreType.DMA((HALF,))] * 2,
+            pltpu.SemaphoreType.DMA((nx - 1,)),
+            *[pltpu.SemaphoreType.DMA((HALF,))] * 2,
+            pltpu.SemaphoreType.DMA((3 + nx,)),
         ]
 
     scratch = [
@@ -524,7 +497,7 @@
             out_shape=(rows, rows, rows),
             in_specs=[pl.BlockSpec(memory_space=pl.ANY)] * 3,
             out_specs=[pl.BlockSpec(memory_space=pl.ANY)] * 3,
-            scratch_shapes=[pltpu.SemaphoreType.DMA((3,))],
+            scratch_shapes=[*[pltpu.VMEM((DIM, width), BF16)] * 3, pltpu.SemaphoreType.DMA((2, 3))],
             compiler_params=pltpu.CompilerParams(vmem_limit_bytes=62 * 1024 * 1024),
         )(dq, dk, dv)
         share = rx * DIM // (2 * nz)

time: 160 us -> 82.1 us (0.51)
  Pallas kernels: 158 us -> 79.9 us
    pallas_call x1, Pallas kernels: 48.8 us -> 2.23 us  [body(): pl.pallas_call(hand_over, out_shape=(rows, rows, rows), in_specs=[pl.Bloc...]
    pallas_call x1, Pallas kernels: 109 us -> 77.6 us  [body(): pl.pallas_call(functools.partial(kernel, (ny, nx, nz)), out_shape=(rows,...]
where the time goes in v3:
time: 82.1 us; the launch traced here: 81.8 us
  Pallas kernels  79.9 us (97%)
  local copies, waits for them, and re-layouts  1.24 us (2%)
    pallas_call x1, Pallas kernels, body(): pl.pallas_call(functools.partial(kernel, (ny, nx, nz)), out_shape=(rows,...  77.6 us
    pallas_call x1, Pallas kernels, body(): pl.pallas_call(hand_over, out_shape=(rows, rows, rows), in_specs=[pl.Bloc...  2.23 us

profile of v3, /device:TPU:1, one launch (start us, length us, event | category | flops | bytes accessed | tf_op | source)
XLA Modules:
  0.0 81.8 jit_solution(12280071229905672933)
XLA Ops:
  0.6 77.6 %shard_map.84 = (bf16[1,128,2048]{2,1,0:T(8,128)(2,1)}, bf16[1,128,2048]{2,1,0:T(8,128)(2,1)}, bf16[1,128,2048]{2,1,0:T(8,128)(2,1)}, f32[1,128]{1,0:T(1,128)}) custom-call(bf16[1,128,2048]{2,1,0:T(8,128)(2,1)} %q_hbm.1, bf16[1,128,2048]{2,1,0:T(8,128)(2,1)} %k_hbm.1, bf16[1,128,2048]{2,1,0:T(8,128)(2,1)} %v_hbm.1, bf16[1,128,2048]{2,1,0:T(8,128)(2,1)} %g_hbm.1, ...), custom_call_target="tpu_custom_call" | custom-call | tf_op jit(solution)/shard_map/pallas_call | solution.py:485
  78.3 0.0 copy-start
  78.3 0.7 copy-done
  78.9 0.6 dynamic-slice_bitcast_fusion
  79.5 2.2 %shard_map.85 = (bf16[1,128,2048]{2,1,0:T(8,128)(2,1)}, bf16[1,128,2048]{2,1,0:T(8,128)(2,1)}, bf16[1,128,2048]{2,1,0:T(8,128)(2,1)}) custom-call(bf16[1,128,2048]{2,1,0:T(8,128)(2,1)} %get-tuple-element.11.a, bf16[1,128,2048]{2,1,0:T(8,128)(2,1)} %get-tuple-element.12.b, bf16[1,128,2048]{2,1,0:T(8,128)(2,1)} %get-tuple-element.13.c), custom_call_target="tpu_custom_call" | custom-call | tf_op jit(solution)/shard_map/pallas_call | solution.py:495
Async XLA Ops:
  78.3 0.7 copy-start

commit v4 on v3

--- a/solution.py
+++ b/solution.py
@@ -18,14 +18,26 @@
 
 LAG = 2
 SUM_LAG = 2
+BLOCK = 32
 
 
 def dot(a, b, ca, cb):
     return lax.dot_general(a, b, (((ca,), (cb,)), ((), ())), preferred_element_type=F32)
 
 
-def turn(e):
-    return 4 - e // 2 + (e % 2) * (e // 2 + (e + 1) // 2)
+def listed(places, e):
+    packed = sum(place << (3 * i) for i, place in enumerate(places))
+    return lax.shift_right_logical(jnp.int32(packed), jnp.int32(3) * e) % 8
+
+
+MAKE = (4, 5, 3, 6, 2, 7, 1, 0)
+SEND = (5, 3, 6, 2, 7, 1)
+WORK = (5, 0, 3, 4, 6, 2, 7, 1)
+
+
+def ring(places, e, z, nz):
+    away = listed(places, e)
+    return (z + away + (z % 2) * (nz - 2 * away)) % nz
 
 
 class Scan:
@@ -33,12 +45,14 @@
         self.nx, self.nz = sizes
         self.y, self.x, self.z, self.c = pos
         self.order = order
-        if order > 0:
-            self.px, self.pc = self.x, self.c
-        else:
-            self.px, self.pc = self.nx - 1 - self.x, 1 - self.c
-        self.own, self.exch, self.s, self.gin, self.r, self.rin, self.pout, self.pin, self.bkin, self.bkout = bufs
-        self.re, self.ri, self.rx, self.ro, self.rb, self.sends = sems
+        self.pc = self.c if order > 0 else 1 - self.c
+        self.slot = self.x * self.nz + self.z
+        self.mate = self.z + 1 - 2 * (self.z % 2)
+        self.first = self.z % 2 == (0 if order > 0 else 1)
+        self.far = (self.z + self.nz // 2) % self.nz
+        self.passed = (self.mate + self.nz // 2) % self.nz
+        (self.own, self.exch, self.s, self.gin, self.pout, self.pin, self.bkin, self.bkout, self.given, self.both, self.on) = bufs
+        self.re, self.ri, self.ro, self.rb, self.rg, self.sends = sems
 
     def device(self, x, z, c):
         return (self.y, (x * self.nz + z) * 2 + c)
@@ -54,72 +68,96 @@
     def exch_copy(self, m):
         return self.remote(self.own.at[(1 - self.c) * HALF + m], self.exch.at[m], 0, self.re.at[m], self.partner())
 
-    def in_copy(self, m, slot):
-        return self.remote(self.s.at[m], self.gin.at[slot], 1, self.ri.at[slot], self.device(self.x, m, self.c))
-
-    def out_copy(self, m, slot):
-        return self.remote(self.pout.at[m], self.pin.at[slot], 2, self.ro.at[slot], self.device(self.x, m, self.c))
+    def clear(self):
+        for x in range(self.nx):
+            self.gin[x * self.nz + self.far] = jnp.zeros((DIM // self.nx, DIM), F32)
+
+    def give_copy(self):
+        to = self.device(self.x, self.mate, self.c)
+        return self.remote(self.s.at[self.far], self.given, 4, self.rg, to)
+
+    def on_copy(self):
+        to = self.device(self.x, self.mate, self.c)
+        return self.remote(self.on, self.pin.at[self.passed], 5, self.ro.at[self.passed], to)
+
+    def in_copy(self, src, m, r):
+        return self.remote(src.at[r], self.gin.at[self.slot], 1, self.ri, self.device(r, m, self.c))
+
+    def out_copy(self, x, z):
+        to = self.device(x, z, self.c)
+        return self.remote(self.pout.at[x * self.nz + z], self.pin.at[self.z, self.x], 2, self.ro.at[self.z], to)
 
     def bk_copy(self, m):
         return self.remote(self.bkout.at[m], self.bkin.at[m], 3, self.rb.at[m], self.partner())
 
-    def x_copy(self, i):
-        to = self.device(self.x + i * self.order, self.z, self.c)
-        return self.remote(self.r, self.rin.at[i - 1], 3 + i, self.rx.at[i - 1], to)
-
     def add_chip(self, m):
         self.exch_copy(m).wait_recv()
-        total = self.own[self.c * HALF + m] + self.exch[m]
-
+        parts = (self.nx, DIM // self.nx, DIM)
+        self.s[m] = (self.own[self.c * HALF + m] + self.exch[m]).reshape(parts)
+
+        @pl.when(m == self.far)
+        def _():
+            self.give_copy().start()
+
+        @pl.when((m != self.far) & (m != self.passed))
+        def _():
+            for i in range(1, self.nx):
+                self.in_copy(self.s.at[m], m, (self.x + i) % self.nx).start()
+
+            @pl.when(m == self.z)
+            def _():
+                self.gin[self.slot] = self.s[m, self.x]
+
+            @pl.when(m != self.z)
+            def _():
+                self.in_copy(self.s.at[m], m, self.x).start()
+
+    def pass_in(self):
+        self.give_copy().wait_recv()
+        self.both[...] = self.s[self.passed] + self.given[...]
+        for r in range(self.nx):
+            self.in_copy(self.both, self.passed, r).start()
+
+    def scan(self):
+        slots = self.nx * self.nz
+        some = pl.ds(0, slots - self.nx - 1)
+        self.remote(self.gin.at[some], self.gin.at[some], 1, self.ri, self.partner()).wait_recv()
+        total = jnp.zeros((DIM // self.nx, DIM), F32)
+        for i in range(slots):
+            slot = i if self.order > 0 else slots - 1 - i
+            self.pout[slot] = total
+            total = total + self.gin[slot]
+        self.pin[self.z, self.x] = self.pout[self.slot]
+
+        @pl.loop(0, self.nz - 2)
+        def _(e):
+            for i in range(self.nx):
+                self.out_copy((self.x + i) % self.nx, ring(SEND, e, self.z, self.nz)).start()
+
+        for i in range(1, self.nx):
+            self.out_copy((self.x + i) % self.nx, self.z).start()
+
+    def arrived(self, m, parts):
+        part = self.pin.at[m, pl.ds(0, parts)]
+        self.remote(part, part, 2, self.ro.at[m], self.partner()).wait_recv()
+
+    def finish(self, m):
         @pl.when(m == self.z)
         def _():
-            self.gin[m] = total
+            self.arrived(m, self.nx - 1)
 
         @pl.when(m != self.z)
         def _():
-            self.s[m] = total
-            self.in_copy(m, self.z).start()
-
-    def add_row(self):
-        for e in range(self.nz - 1):
-            source = (self.z + self.nz - turn(e)) % self.nz
-            self.in_copy(source, source).wait_recv()
-        total = self.gin[0]
-        for m in range(1, self.nz):
-            total = total + self.gin[m]
-        self.r[...] = total
-        for i in range(1, self.nx):
-
-            @pl.when(self.px + i < self.nx)
-            def _(i=i):
-                self.x_copy(i).start()
-
-    def spread(self):
-        self.pout[0] = jnp.zeros((DIM, DIM), F32)
-        for i in range(1, self.nx):
-
-            @pl.when(self.px >= i)
-            def _(i=i):
-                self.x_copy(i).wait_recv()
-                self.pout[0] = self.pout[0] + self.rin[i - 1]
-
-        total = self.pout[0]
-        for m in range(self.nz):
-            place = m if self.order > 0 else self.nz - 1 - m
-            self.pout[place] = total
-            total = total + self.gin[place]
-        self.pin[self.z] = self.pout[self.z]
-
-        @pl.loop(0, self.nz - 1)
-        def _(e):
-            self.out_copy((self.z + turn(e)) % self.nz, self.z).start()
-
-    def finish(self, m):
-        @pl.when(m != self.z)
+            self.arrived(m, self.nx)
+
+        @pl.when(m == self.passed)
         def _():
-            self.out_copy(m, m).wait_recv()
-
-        before = self.pin[m]
+            before = self.pin[m]
+            self.on[...] = jnp.where(self.first, before + self.s[m], before)
+            self.on_copy().start()
+            self.pin[m] = jnp.where(self.first, before, before + self.given[...])
+
+        before = self.pin[m].reshape(DIM, DIM)
         self.bkout[m] = jnp.where(self.pc == 0, before + self.own[self.c * HALF + m], before)
         self.bk_copy(m).start()
         return jnp.where(self.pc == 1, before + self.exch[m], before)
@@ -129,16 +167,13 @@
         return self.bkin[m]
 
     def drain(self):
-        some = pl.ds(0, self.nz - 1)
+        some = pl.ds(0, self.nx * (self.nz - 1) - 1)
         self.remote(self.exch, self.exch, 0, self.re.at[0], self.partner()).wait_send()
-        self.remote(self.s.at[some], self.gin.at[some], 1, self.ri.at[0], self.partner()).wait_send()
-        self.remote(self.pout.at[some], self.pin.at[some], 2, self.ro.at[0], self.partner()).wait_send()
+        self.remote(self.gin.at[some], self.gin.at[some], 1, self.ri, self.partner()).wait_send()
+        self.remote(self.pout.at[some], self.pout.at[some], 2, self.ro.at[0], self.partner()).wait_send()
         self.remote(self.bkout, self.bkin, 3, self.rb.at[0], self.partner()).wait_send()
-        for i in range(1, self.nx):
-
-            @pl.when(self.px + i < self.nx)
-            def _(i=i):
-                self.x_copy(i).wait_send()
+        self.give_copy().wait_send()
+        self.on_copy().wait_send()
 
 
 def kernel(
@@ -167,8 +202,8 @@
     scores, d_out, prior = take(3)
     out_loc, dk_loc, dv_loc = take(3)
     gtile, gin1, acc1, gin2, acc2, gin3, acc3, gin4 = take(8)
-    bufs1, sems1 = take(10), take(6)
-    bufs2, sems2 = take(10), take(6)
+    bufs1, sems1 = take(11), take(6)
+    bufs2, sems2 = take(11), take(6)
     in_sem, out_sem, gsend, g1r, g2r, g3r, g4r = take(7)
 
     y = lax.axis_index("dp")
@@ -197,12 +232,18 @@
     partner = device(y, x, z, 1 - c)
     barrier = pltpu.get_barrier_semaphore()
     pl.semaphore_signal(barrier, inc=1, device_id=partner, device_id_type=MESH)
-    for count, peer in ((ny, y_peer), (nx, x_peer), (nz, z_peer)):
-        for i in range(1, count):
-            pl.semaphore_signal(barrier, inc=1, device_id=peer(i), device_id_type=MESH)
+    for i in range(1, ny):
+        pl.semaphore_signal(barrier, inc=1, device_id=y_peer(i), device_id_type=MESH)
+
+    @pl.loop(1, nx * nz)
+    def _(i):
+        to = (x * nz + z + i) % (nx * nz)
+        pl.semaphore_signal(barrier, inc=1, device_id=(y, to * 2 + c), device_id_type=MESH)
 
     one = Scan((nx, nz), pos, 1, bufs1, sems1)
     two = Scan((nx, nz), pos, -1, bufs2, sems2)
+    one.clear()
+    two.clear()
 
     def col(h):
         return pl.ds(pl.multiple_of(h * DIM, DIM), DIM)
@@ -222,12 +263,12 @@
     loads[1].wait()
 
     def place(e):
-        return (z + turn(e)) % nz
+        return ring(MAKE, jnp.int32(e), z, nz)
 
     for i in range(0, HALF, 4):
         local_states([other + place(i + u) for u in range(4)])
         if i == 0:
-            pl.semaphore_wait(barrier, ny + nx + nz - 2)
+            pl.semaphore_wait(barrier, nx * nz + ny - 1)
         for u in range(4):
             one.exch_copy(place(i + u)).start()
 
@@ -235,6 +276,7 @@
         local_states([mine + place(i + u) for u in range(4)])
         for u in range(4):
             one.add_chip(place(i + u))
+    one.pass_in()
 
     loads[2].wait()
     loads[3].wait()
@@ -354,17 +396,22 @@
         else:
             g4_copy().wait_recv()
             scale = 1.0 / math.sqrt(ny * nx * nz * 2 * DIM)
-            dgain_ref[...] = jnp.sum(acc3[...] + gin4[...], axis=1) * scale
+            total = jnp.sum(acc3[...] + gin4[...], axis=1, keepdims=True) * scale
+            dgain_ref[...] = jnp.broadcast_to(total, dgain_ref.shape)
 
     def arrival(e):
-        return (z + nz - turn((e + nz - 1) % nz)) % nz
-
-    def finishing(scan, work, after, last):
+        return ring(WORK, e, z, nz)
+
+    def finishing(scan, work, after, last, final):
         @pl.loop(0, HALF + LAG + SUM_LAG)
         def _(e):
             @pl.when(e >= LAG + SUM_LAG)
             def _():
                 last(arrival(e - LAG - SUM_LAG))
+
+            @pl.when(e == HALF + LAG)
+            def _():
+                final()
 
             @pl.when(e < LAG)
             def _():
@@ -384,16 +431,15 @@
                 work([other + n], [scan.finished(n)])
                 after(n)
 
-    def nothing(m):
+    def nothing(*_):
         pass
 
     @pl.loop(0, HALF)
     def _(m):
         before_one([mine + m, other + m])
 
-    one.add_row()
-    one.spread()
-    finishing(one, pass_one, lambda m: two.exch_copy(m).start(), two.add_chip)
+    one.scan()
+    finishing(one, pass_one, lambda m: two.exch_copy(m).start(), two.add_chip, two.pass_in)
     gain_step(0)
 
     @pl.loop(0, HALF)
@@ -406,10 +452,9 @@
 
     pltpu.make_async_copy(dq, dq_hbm.at[0], out_sem.at[0]).start()
     gain_step(2)
-    two.add_row()
-    two.spread()
+    two.scan()
     gain_step(3)
-    finishing(two, pass_two, nothing, nothing)
+    finishing(two, pass_two, nothing, nothing, nothing)
     gain_step(4)
 
     one.drain()
@@ -425,12 +470,23 @@
         pltpu.make_async_copy(ref, hbm.at[0], out_sem.at[i]).wait()
 
 
-def hand_over(a, b, c, a_out, b_out, c_out, a_buf, b_buf, c_buf, sems):
+def hand_over(nz, a, b, c, gain, a_out, b_out, c_out, gain_out, a_buf, b_buf, c_buf, gain_buf, sems):
     trips = ((a, a_buf, a_out), (b, b_buf, b_out), (c, c_buf, c_out))
-    loads = [pltpu.make_async_copy(src.at[0], buf, sems.at[0, i]) for i, (src, buf, _) in enumerate(trips)]
-    stores = [pltpu.make_async_copy(buf, dst.at[0], sems.at[1, i]) for i, (_, buf, dst) in enumerate(trips)]
+    loads, stores = [], []
+    for row in range(0, DIM, BLOCK):
+        for src, buf, dst in trips:
+            part, i = pl.ds(row, BLOCK), len(loads)
+            loads.append(pltpu.make_async_copy(src.at[0, part], buf.at[part], sems.at[0, i]))
+            stores.append(pltpu.make_async_copy(buf.at[part], dst.at[0, part], sems.at[1, i]))
+    load_gain = pltpu.make_async_copy(gain, gain_buf, sems.at[0, len(loads)])
+    load_gain.start()
     for load in loads:
         load.start()
+    load_gain.wait()
+    share = gain_out.shape[1]
+    place = lax.rem(lax.axis_index("ctx"), 2 * nz) * share
+    turned = pltpu.roll(gain_buf[place // DIM], (DIM - place % DIM) % DIM, 1)
+    gain_out[...] = turned[0:1, :share]
     for load, store in zip(loads, stores):
         load.wait()
         store.start()
@@ -445,16 +501,23 @@
 
     def scan_scratch():
         state = pltpu.VMEM((HALF, DIM, DIM), F32)
+        parts = pltpu.VMEM((HALF, nx, DIM // nx, DIM), F32)
+        slots = pltpu.VMEM((nx * nz, DIM // nx, DIM), F32)
         return [
             pltpu.VMEM((HEADS, DIM, DIM), F32),
-            *[state] * 3,
-            pltpu.VMEM((DIM, DIM), F32),
-            pltpu.VMEM((nx - 1, DIM, DIM), F32),
-            *[state] * 4,
+            state,
+            parts,
+            slots,
+            slots,
+            parts,
+            state,
+            state,
+            *[pltpu.VMEM((nx, DIM // nx, DIM), F32)] * 3,
+            pltpu.SemaphoreType.DMA((HALF,)),
+            pltpu.SemaphoreType.DMA,
             *[pltpu.SemaphoreType.DMA((HALF,))] * 2,
-            pltpu.SemaphoreType.DMA((nx - 1,)),
-            *[pltpu.SemaphoreType.DMA((HALF,))] * 2,
-            pltpu.SemaphoreType.DMA((3 + nx,)),
+            pltpu.SemaphoreType.DMA,
+            pltpu.SemaphoreType.DMA((6,)),
         ]
 
     scratch = [
@@ -484,7 +547,7 @@
         rows = jax.ShapeDtypeStruct(queries.shape, BF16)
         dq, dk, dv, dgain = pl.pallas_call(
             functools.partial(kernel, (ny, nx, nz)),
-            out_shape=(rows, rows, rows, jax.ShapeDtypeStruct((rx, DIM), F32)),
+            out_shape=(rows, rows, rows, jax.ShapeDtypeStruct((rx, 8, DIM), F32)),
             in_specs=[pl.BlockSpec(memory_space=pl.ANY)] * 4 + [pl.BlockSpec(memory_space=pltpu.VMEM)],
             out_specs=[pl.BlockSpec(memory_space=pl.ANY)] * 3 + [pl.BlockSpec(memory_space=pltpu.VMEM)],
             scratch_shapes=scratch,
@@ -492,17 +555,20 @@
                 collective_id=0, has_side_effects=True, vmem_limit_bytes=62 * 1024 * 1024
             ),
         )(queries, key_rows, value_rows, out_grad, norm_gain.reshape(1, width))
-        dq, dk, dv = pl.pallas_call(
-            hand_over,
-            out_shape=(rows, rows, rows),
-            in_specs=[pl.BlockSpec(memory_space=pl.ANY)] * 3,
-            out_specs=[pl.BlockSpec(memory_space=pl.ANY)] * 3,
-            scratch_shapes=[*[pltpu.VMEM((DIM, width), BF16)] * 3, pltpu.SemaphoreType.DMA((2, 3))],
+        share = rx * DIM // (2 * nz)
+        dq, dk, dv, dgain = pl.pallas_call(
+            functools.partial(hand_over, nz),
+            out_shape=(rows, rows, rows, jax.ShapeDtypeStruct((1, share), F32)),
+            in_specs=[pl.BlockSpec(memory_space=pl.ANY)] * 4,
+            out_specs=[pl.BlockSpec(memory_space=pl.ANY)] * 3 + [pl.BlockSpec(memory_space=pltpu.VMEM)],
+            scratch_shapes=[
+                *[pltpu.VMEM((DIM, width), BF16)] * 3,
+                pltpu.VMEM((rx, 8, DIM), F32),
+                pltpu.SemaphoreType.DMA((2, 3 * (DIM // BLOCK) + 1)),
+            ],
             compiler_params=pltpu.CompilerParams(vmem_limit_bytes=62 * 1024 * 1024),
-        )(dq, dk, dv)
-        share = rx * DIM // (2 * nz)
-        place = lax.rem(lax.axis_index("ctx"), 2 * nz) * share
-        return dq, dk, dv, lax.dynamic_slice(dgain.reshape(rx * DIM), (place,), (share,))
+        )(dq, dk, dv, dgain)
+        return dq, dk, dv, dgain.reshape(share)
 
     placed = P("dp", "ctx", None)
     return jax.shard_map(

time: 82.1 us -> 75.8 us (0.923)
  Pallas kernels: 79.9 us -> 75 us
  local copies, waits for them, and re-layouts: 1.24 us -> 0 us
    pallas_call x1, Pallas kernels: 77.6 us -> 72.1 us  [body(): pl.pallas_call(functools.partial(kernel, (ny, nx, nz)), out_shape=(rows,...]
where the time goes in v4:
time: 75.8 us; the launch traced here: 75.6 us
  Pallas kernels  75 us (99%)
    pallas_call x1, Pallas kernels, body(): pl.pallas_call(functools.partial(kernel, (ny, nx, nz)), out_shape=(rows,...  72.1 us
    pallas_call x1, Pallas kernels, body(): pl.pallas_call(functools.partial(hand_over, nz), out_shape=(rows, rows, r...  2.86 us

profile of v4, /device:TPU:1, one launch (start us, length us, event | category | flops | bytes accessed | tf_op | source)
XLA Modules:
  0.0 75.6 jit_solution(13635095063555947841)
XLA Ops:
  0.6 72.1 %shard_map.84 = (bf16[1,128,2048]{2,1,0:T(8,128)(2,1)}, bf16[1,128,2048]{2,1,0:T(8,128)(2,1)}, bf16[1,128,2048]{2,1,0:T(8,128)(2,1)}, f32[1,8,128]{2,1,0:T(8,128)}) custom-call(bf16[1,128,2048]{2,1,0:T(8,128)(2,1)} %q_hbm.1, bf16[1,128,2048]{2,1,0:T(8,128)(2,1)} %k_hbm.1, bf16[1,128,2048]{2,1,0:T(8,128)(2,1)} %v_hbm.1, bf16[1,128,2048]{2,1,0:T(8,128)(2,1)} %g_hbm.1, ...), custom_call_target="tpu_custom_call" | custom-call | tf_op jit(solution)/shard_map/pallas_call | solution.py:548
  72.8 2.9 %shard_map.85 = (bf16[1,128,2048]{2,1,0:T(8,128)(2,1)}, bf16[1,128,2048]{2,1,0:T(8,128)(2,1)}, bf16[1,128,2048]{2,1,0:T(8,128)(2,1)}, f32[1,8]{1,0:T(1,128)}) custom-call(bf16[1,128,2048]{2,1,0:T(8,128)(2,1)} %get-tuple-element.12.a, bf16[1,128,2048]{2,1,0:T(8,128)(2,1)} %get-tuple-element.13.b, bf16[1,128,2048]{2,1,0:T(8,128)(2,1)} %get-tuple-element.14.c, ...), custom_call_target="tpu_custom_call" | custom-call | tf_op jit(solution)/shard_map/pallas_call | solution.py:559

commit v5 on v4

--- a/solution.py
+++ b/solution.py
@@ -18,6 +18,8 @@
 
 LAG = 2
 SUM_LAG = 2
+EARLY_ONE = 5
+EARLY_TWO = 4
 BLOCK = 32
 
 
@@ -402,9 +404,11 @@
     def arrival(e):
         return ring(WORK, e, z, nz)
 
-    def finishing(scan, work, after, last, final):
+    def finishing(scan, work, after, last, final, fill):
         @pl.loop(0, HALF + LAG + SUM_LAG)
         def _(e):
+            fill(e)
+
             @pl.when(e >= LAG + SUM_LAG)
             def _():
                 last(arrival(e - LAG - SUM_LAG))
@@ -434,27 +438,46 @@
     def nothing(*_):
         pass
 
-    @pl.loop(0, HALF)
-    def _(m):
-        before_one([mine + m, other + m])
+    def pair(work, e):
+        m = arrival(e)
+        work([mine + m, other + m])
+
+    @pl.loop(0, EARLY_ONE)
+    def _(e):
+        pair(before_one, e)
 
     one.scan()
-    finishing(one, pass_one, lambda m: two.exch_copy(m).start(), two.add_chip, two.pass_in)
+
+    def fill_one(e):
+        @pl.when(e < HALF - EARLY_ONE)
+        def _():
+            pair(before_one, e + EARLY_ONE)
+
+    finishing(one, pass_one, lambda m: two.exch_copy(m).start(), two.add_chip, two.pass_in, fill_one)
     gain_step(0)
 
-    @pl.loop(0, HALF)
-    def _(m):
-        between([mine + m, other + m])
-
-        @pl.when(m == HALF // 2)
-        def _():
-            gain_step(1)
-
-    pltpu.make_async_copy(dq, dq_hbm.at[0], out_sem.at[0]).start()
-    gain_step(2)
+    @pl.loop(0, EARLY_TWO)
+    def _(e):
+        pair(between, e)
+
     two.scan()
-    gain_step(3)
-    finishing(two, pass_two, nothing, nothing, nothing)
+    gain_step(1)
+
+    def fill_two(e):
+        @pl.when(e < HALF - EARLY_TWO)
+        def _():
+            pair(between, e + EARLY_TWO)
+
+        @pl.when(e == HALF - EARLY_TWO)
+        def _():
+            gain_step(2)
+            pltpu.make_async_copy(dq, dq_hbm.at[0], out_sem.at[0]).start()
+
+        @pl.when(e == HALF)
+        def _():
+            gain_step(3)
+
+    finishing(two, pass_two, nothing, nothing, nothing, fill_two)
     gain_step(4)
 
     one.drain()

time: 75.8 us -> 77 us (1.016)
  Pallas kernels: 75 us -> 76.2 us
    pallas_call x1, Pallas kernels: 72.1 us -> 73.4 us  [body(): pl.pallas_call(functools.partial(kernel, (ny, nx, nz)), out_shape=(rows,...]
where the time goes in v5:
time: 77 us; the launch traced here: 76.9 us
  Pallas kernels  76.2 us (99%)
    pallas_call x1, Pallas kernels, body(): pl.pallas_call(functools.partial(kernel, (ny, nx, nz)), out_shape=(rows,...  73.4 us
    pallas_call x1, Pallas kernels, body(): pl.pallas_call(functools.partial(hand_over, nz), out_shape=(rows, rows, r...  2.86 us

profile of v5, /device:TPU:1, one launch (start us, length us, event | category | flops | bytes accessed | tf_op | source)
XLA Modules:
  0.0 76.9 jit_solution(15300904895476097501)
XLA Ops:
  0.6 73.4 %shard_map.84 = (bf16[1,128,2048]{2,1,0:T(8,128)(2,1)}, bf16[1,128,2048]{2,1,0:T(8,128)(2,1)}, bf16[1,128,2048]{2,1,0:T(8,128)(2,1)}, f32[1,8,128]{2,1,0:T(8,128)}) custom-call(bf16[1,128,2048]{2,1,0:T(8,128)(2,1)} %q_hbm.1, bf16[1,128,2048]{2,1,0:T(8,128)(2,1)} %k_hbm.1, bf16[1,128,2048]{2,1,0:T(8,128)(2,1)} %v_hbm.1, bf16[1,128,2048]{2,1,0:T(8,128)(2,1)} %g_hbm.1, ...), custom_call_target="tpu_custom_call" | custom-call | tf_op jit(solution)/shard_map/pallas_call | solution.py:571
  74.0 2.9 %shard_map.85 = (bf16[1,128,2048]{2,1,0:T(8,128)(2,1)}, bf16[1,128,2048]{2,1,0:T(8,128)(2,1)}, bf16[1,128,2048]{2,1,0:T(8,128)(2,1)}, f32[1,8]{1,0:T(1,128)}) custom-call(bf16[1,128,2048]{2,1,0:T(8,128)(2,1)} %get-tuple-element.12.a, bf16[1,128,2048]{2,1,0:T(8,128)(2,1)} %get-tuple-element.13.b, bf16[1,128,2048]{2,1,0:T(8,128)(2,1)} %get-tuple-element.14.c, ...), custom_call_target="tpu_custom_call" | custom-call | tf_op jit(solution)/shard_map/pallas_call | solution.py:582

commit v6 on v4

--- a/solution.py
+++ b/solution.py
@@ -470,26 +470,21 @@
         pltpu.make_async_copy(ref, hbm.at[0], out_sem.at[i]).wait()
 
 
-def hand_over(nz, a, b, c, gain, a_out, b_out, c_out, gain_out, a_buf, b_buf, c_buf, gain_buf, sems):
-    trips = ((a, a_buf, a_out), (b, b_buf, b_out), (c, c_buf, c_out))
-    loads, stores = [], []
+def hand_over(nz, a, b, c, gain, a_out, b_out, c_out, gain_out, gain_buf, sems):
+    stores = []
     for row in range(0, DIM, BLOCK):
-        for src, buf, dst in trips:
-            part, i = pl.ds(row, BLOCK), len(loads)
-            loads.append(pltpu.make_async_copy(src.at[0, part], buf.at[part], sems.at[0, i]))
-            stores.append(pltpu.make_async_copy(buf.at[part], dst.at[0, part], sems.at[1, i]))
-    load_gain = pltpu.make_async_copy(gain, gain_buf, sems.at[0, len(loads)])
+        for src, dst in ((a, a_out), (b, b_out), (c, c_out)):
+            part = pl.ds(row, BLOCK)
+            stores.append(pltpu.make_async_copy(src.at[0, part], dst.at[0, part], sems.at[len(stores)]))
+    load_gain = pltpu.make_async_copy(gain, gain_buf, sems.at[len(stores)])
     load_gain.start()
-    for load in loads:
-        load.start()
+    for store in stores:
+        store.start()
     load_gain.wait()
     share = gain_out.shape[1]
     place = lax.rem(lax.axis_index("ctx"), 2 * nz) * share
     turned = pltpu.roll(gain_buf[place // DIM], (DIM - place % DIM) % DIM, 1)
     gain_out[...] = turned[0:1, :share]
-    for load, store in zip(loads, stores):
-        load.wait()
-        store.start()
     for store in stores:
         store.wait()
 
@@ -547,7 +542,7 @@
         rows = jax.ShapeDtypeStruct(queries.shape, BF16)
         dq, dk, dv, dgain = pl.pallas_call(
             functools.partial(kernel, (ny, nx, nz)),
-            out_shape=(rows, rows, rows, jax.ShapeDtypeStruct((rx, 8, DIM), F32)),
+            out_shape=(*[pltpu.VMEM(queries.shape, BF16)] * 3, pltpu.VMEM((rx, 8, DIM), F32)),
             in_specs=[pl.BlockSpec(memory_space=pl.ANY)] * 4 + [pl.BlockSpec(memory_space=pltpu.VMEM)],
             out_specs=[pl.BlockSpec(memory_space=pl.ANY)] * 3 + [pl.BlockSpec(memory_space=pltpu.VMEM)],
             scratch_shapes=scratch,
@@ -561,12 +556,8 @@
             out_shape=(rows, rows, rows, jax.ShapeDtypeStruct((1, share), F32)),
             in_specs=[pl.BlockSpec(memory_space=pl.ANY)] * 4,
             out_specs=[pl.BlockSpec(memory_space=pl.ANY)] * 3 + [pl.BlockSpec(memory_space=pltpu.VMEM)],
-            scratch_shapes=[
-                *[pltpu.VMEM((DIM, width), BF16)] * 3,
-                pltpu.VMEM((rx, 8, DIM), F32),
-                pltpu.SemaphoreType.DMA((2, 3 * (DIM // BLOCK) + 1)),
-            ],
-            compiler_params=pltpu.CompilerParams(vmem_limit_bytes=62 * 1024 * 1024),
+            scratch_shapes=[pltpu.VMEM((rx, 8, DIM), F32), pltpu.SemaphoreType.DMA((3 * (DIM // BLOCK) + 1,))],
+            compiler_params=pltpu.CompilerParams(vmem_limit_bytes=8 * 1024 * 1024),
         )(dq, dk, dv, dgain)
         return dq, dk, dv, dgain.reshape(share)
 

time: 75.8 us -> 73.7 us (0.972)
  Pallas kernels: 75 us -> 72.9 us
    pallas_call x1, Pallas kernels: 2.86 us -> 1.76 us  [body(): pl.pallas_call(functools.partial(hand_over, nz), out_shape=(rows, rows, r...]
    pallas_call x1, Pallas kernels: 72.1 us -> 71.2 us  [body(): pl.pallas_call(functools.partial(kernel, (ny, nx, nz)), out_shape=(*[pltp...]
where the time goes in v6:
time: 73.7 us; the launch traced here: 73.6 us
  Pallas kernels  72.9 us (99%)
    pallas_call x1, Pallas kernels, body(): pl.pallas_call(functools.partial(kernel, (ny, nx, nz)), out_shape=(*[pltp...  71.2 us
    pallas_call x1, Pallas kernels, body(): pl.pallas_call(functools.partial(hand_over, nz), out_shape=(rows, rows, r...  1.76 us

profile of v6, /device:TPU:1, one launch (start us, length us, event | category | flops | bytes accessed | tf_op | source)
XLA Modules:
  0.0 73.6 jit_solution(6849876107549508051)
XLA Ops:
  0.6 71.2 %shard_map.84 = (bf16[1,128,2048]{2,1,0:T(8,128)(2,1)S(1)}, bf16[1,128,2048]{2,1,0:T(8,128)(2,1)S(1)}, bf16[1,128,2048]{2,1,0:T(8,128)(2,1)S(1)}, f32[1,8,128]{2,1,0:T(8,128)S(1)}) custom-call(bf16[1,128,2048]{2,1,0:T(8,128)(2,1)} %q_hbm.1, bf16[1,128,2048]{2,1,0:T(8,128)(2,1)} %k_hbm.1, bf16[1,128,2048]{2,1,0:T(8,128)(2,1)} %v_hbm.1, ...), custom_call_target="tpu_custom_call" | custom-call | tf_op jit(solution)/shard_map/pallas_call | solution.py:543
  71.8 1.8 %shard_map.85 = (bf16[1,128,2048]{2,1,0:T(8,128)(2,1)}, bf16[1,128,2048]{2,1,0:T(8,128)(2,1)}, bf16[1,128,2048]{2,1,0:T(8,128)(2,1)}, f32[1,8]{1,0:T(1,128)}) custom-call(bf16[1,128,2048]{2,1,0:T(8,128)(2,1)S(1)} %get-tuple-element.12.a, bf16[1,128,2048]{2,1,0:T(8,128)(2,1)S(1)} %get-tuple-element.13.b, bf16[1,128,2048]{2,1,0:T(8,128)(2,1)S(1)} %get-tuple-element.14.c, ...), custom_call_target="tpu_custom_call" | custom-call | tf_op jit(solution)/shard_map/pallas_call | solution.py:554

commit v7 on v6

--- a/solution.py
+++ b/solution.py
@@ -47,6 +47,10 @@
         self.order = order
         self.pc = self.c if order > 0 else 1 - self.c
         self.slot = self.x * self.nz + self.z
+        self.parts = self.nx // 2
+        self.scans = self.x % 2 == self.c
+        self.xs = [(self.x + i) % self.nx for i in range(self.nx)]
+        self.base = [(2 * p + self.c) * 2 * self.nz + self.c for p in range(self.parts)]
         self.mate = self.z + 1 - 2 * (self.z % 2)
         self.first = self.z % 2 == (0 if order > 0 else 1)
         self.far = (self.z + self.nz // 2) % self.nz
@@ -70,7 +74,7 @@
 
     def clear(self):
         for x in range(self.nx):
-            self.gin[x * self.nz + self.far] = jnp.zeros((DIM // self.nx, DIM), F32)
+            self.gin[x * self.nz + self.far] = jnp.zeros((DIM // self.parts, DIM), F32)
 
     def give_copy(self):
         to = self.device(self.x, self.mate, self.c)
@@ -80,19 +84,19 @@
         to = self.device(self.x, self.mate, self.c)
         return self.remote(self.on, self.pin.at[self.passed], 5, self.ro.at[self.passed], to)
 
-    def in_copy(self, src, m, r):
-        return self.remote(src.at[r], self.gin.at[self.slot], 1, self.ri, self.device(r, m, self.c))
+    def in_copy(self, src, m, p):
+        return self.remote(src.at[p], self.gin.at[self.slot], 1, self.ri, (self.y, self.base[p] + 2 * m))
 
     def out_copy(self, x, z):
         to = self.device(x, z, self.c)
-        return self.remote(self.pout.at[x * self.nz + z], self.pin.at[self.z, self.x], 2, self.ro.at[self.z], to)
+        return self.remote(self.pout.at[x * self.nz + z], self.pin.at[self.z, self.x // 2], 2, self.ro.at[self.z], to)
 
     def bk_copy(self, m):
         return self.remote(self.bkout.at[m], self.bkin.at[m], 3, self.rb.at[m], self.partner())
 
     def add_chip(self, m):
         self.exch_copy(m).wait_recv()
-        parts = (self.nx, DIM // self.nx, DIM)
+        parts = (self.parts, DIM // self.parts, DIM)
         self.s[m] = (self.own[self.c * HALF + m] + self.exch[m]).reshape(parts)
 
         @pl.when(m == self.far)
@@ -101,54 +105,61 @@
 
         @pl.when((m != self.far) & (m != self.passed))
         def _():
-            for i in range(1, self.nx):
-                self.in_copy(self.s.at[m], m, (self.x + i) % self.nx).start()
-
-            @pl.when(m == self.z)
-            def _():
-                self.gin[self.slot] = self.s[m, self.x]
-
-            @pl.when(m != self.z)
-            def _():
-                self.in_copy(self.s.at[m], m, self.x).start()
+            for p in range(self.parts):
+                here = (m == self.z) & (self.x == 2 * p + self.c)
+
+                @pl.when(here)
+                def _(p=p):
+                    self.gin[self.slot] = self.s[m, p]
+
+                @pl.when(jnp.logical_not(here))
+                def _(p=p):
+                    self.in_copy(self.s.at[m], m, p).start()
 
     def pass_in(self):
         self.give_copy().wait_recv()
         self.both[...] = self.s[self.passed] + self.given[...]
-        for r in range(self.nx):
-            self.in_copy(self.both, self.passed, r).start()
+        for p in range(self.parts):
+            self.in_copy(self.both, self.passed, p).start()
 
     def scan(self):
+        pl.when(self.scans)(self.scan_part)
+
+    def scan_part(self):
         slots = self.nx * self.nz
         some = pl.ds(0, slots - self.nx - 1)
         self.remote(self.gin.at[some], self.gin.at[some], 1, self.ri, self.partner()).wait_recv()
-        total = jnp.zeros((DIM // self.nx, DIM), F32)
+        total = jnp.zeros((DIM // self.parts, DIM), F32)
         for i in range(slots):
             slot = i if self.order > 0 else slots - 1 - i
             self.pout[slot] = total
             total = total + self.gin[slot]
-        self.pin[self.z, self.x] = self.pout[self.slot]
+        self.pin[self.z, self.x // 2] = self.pout[self.slot]
 
         @pl.loop(0, self.nz - 2)
         def _(e):
-            for i in range(self.nx):
-                self.out_copy((self.x + i) % self.nx, ring(SEND, e, self.z, self.nz)).start()
-
-        for i in range(1, self.nx):
-            self.out_copy((self.x + i) % self.nx, self.z).start()
+            to = ring(SEND, e, self.z, self.nz)
+            for x in self.xs:
+                self.out_copy(x, to).start()
+
+        for x in self.xs[1:]:
+            self.out_copy(x, self.z).start()
 
     def arrived(self, m, parts):
         part = self.pin.at[m, pl.ds(0, parts)]
         self.remote(part, part, 2, self.ro.at[m], self.partner()).wait_recv()
 
     def finish(self, m):
-        @pl.when(m == self.z)
-        def _():
-            self.arrived(m, self.nx - 1)
-
-        @pl.when(m != self.z)
-        def _():
-            self.arrived(m, self.nx)
+        here = (m == self.z) & self.scans
+        if self.parts > 1:
+
+            @pl.when(here)
+            def _():
+                self.arrived(m, self.parts - 1)
+
+        @pl.when(jnp.logical_not(here))
+        def _():
+            self.arrived(m, self.parts)
 
         @pl.when(m == self.passed)
         def _():
@@ -167,10 +178,21 @@
         return self.bkin[m]
 
     def drain(self):
+        sent = self.parts * (HALF - 1)
         some = pl.ds(0, self.nx * (self.nz - 1) - 1)
         self.remote(self.exch, self.exch, 0, self.re.at[0], self.partner()).wait_send()
-        self.remote(self.gin.at[some], self.gin.at[some], 1, self.ri, self.partner()).wait_send()
-        self.remote(self.pout.at[some], self.pout.at[some], 2, self.ro.at[0], self.partner()).wait_send()
+
+        @pl.when(self.scans)
+        def _():
+            own = self.gin.at[pl.ds(0, sent - 1)]
+            self.remote(own, own, 1, self.ri, self.partner()).wait_send()
+            self.remote(self.pout.at[some], self.pout.at[some], 2, self.ro.at[0], self.partner()).wait_send()
+
+        @pl.when(jnp.logical_not(self.scans))
+        def _():
+            all_parts = self.gin.at[pl.ds(0, sent)]
+            self.remote(all_parts, all_parts, 1, self.ri, self.partner()).wait_send()
+
         self.remote(self.bkout, self.bkin, 3, self.rb.at[0], self.partner()).wait_send()
         self.give_copy().wait_send()
         self.on_copy().wait_send()
@@ -496,8 +518,9 @@
 
     def scan_scratch():
         state = pltpu.VMEM((HALF, DIM, DIM), F32)
-        parts = pltpu.VMEM((HALF, nx, DIM // nx, DIM), F32)
-        slots = pltpu.VMEM((nx * nz, DIM // nx, DIM), F32)
+        count = nx // 2
+        parts = pltpu.VMEM((HALF, count, DIM // count, DIM), F32)
+        slots = pltpu.VMEM((nx * nz, DIM // count, DIM), F32)
         return [
             pltpu.VMEM((HEADS, DIM, DIM), F32),
             state,
@@ -507,7 +530,7 @@
             parts,
             state,
             state,
-            *[pltpu.VMEM((nx, DIM // nx, DIM), F32)] * 3,
+            *[pltpu.VMEM((count, DIM // count, DIM), F32)] * 3,
             pltpu.SemaphoreType.DMA((HALF,)),
             pltpu.SemaphoreType.DMA,
             *[pltpu.SemaphoreType.DMA((HALF,))] * 2,

time: 73.7 us -> 77.5 us (1.052)
  Pallas kernels: 72.9 us -> 76.7 us
    pallas_call x1, Pallas kernels: 71.2 us -> 74.9 us  [body(): pl.pallas_call(functools.partial(kernel, (ny, nx, nz)), out_shape=(*[pltp...]
where the time goes in v7:
time: 77.5 us; the launch traced here: 77.3 us
  Pallas kernels  76.7 us (99%)
    pallas_call x1, Pallas kernels, body(): pl.pallas_call(functools.partial(kernel, (ny, nx, nz)), out_shape=(*[pltp...  74.9 us
    pallas_call x1, Pallas kernels, body(): pl.pallas_call(functools.partial(hand_over, nz), out_shape=(rows, rows, r...  1.76 us

profile of v7, /device:TPU:1, one launch (start us, length us, event | category | flops | bytes accessed | tf_op | source)
XLA Modules:
  0.0 77.3 jit_solution(5660247554373586794)
XLA Ops:
  0.6 74.9 %shard_map.84 = (bf16[1,128,2048]{2,1,0:T(8,128)(2,1)S(1)}, bf16[1,128,2048]{2,1,0:T(8,128)(2,1)S(1)}, bf16[1,128,2048]{2,1,0:T(8,128)(2,1)S(1)}, f32[1,8,128]{2,1,0:T(8,128)S(1)}) custom-call(bf16[1,128,2048]{2,1,0:T(8,128)(2,1)} %q_hbm.1, bf16[1,128,2048]{2,1,0:T(8,128)(2,1)} %k_hbm.1, bf16[1,128,2048]{2,1,0:T(8,128)(2,1)} %v_hbm.1, ...), custom_call_target="tpu_custom_call" | custom-call | tf_op jit(solution)/shard_map/pallas_call | solution.py:566
  75.6 1.8 %shard_map.85 = (bf16[1,128,2048]{2,1,0:T(8,128)(2,1)}, bf16[1,128,2048]{2,1,0:T(8,128)(2,1)}, bf16[1,128,2048]{2,1,0:T(8,128)(2,1)}, f32[1,8]{1,0:T(1,128)}) custom-call(bf16[1,128,2048]{2,1,0:T(8,128)(2,1)S(1)} %get-tuple-element.12.a, bf16[1,128,2048]{2,1,0:T(8,128)(2,1)S(1)} %get-tuple-element.13.b, bf16[1,128,2048]{2,1,0:T(8,128)(2,1)S(1)} %get-tuple-element.14.c, ...), custom_call_target="tpu_custom_call" | custom-call | tf_op jit(solution)/shard_map/pallas_call | solution.py:577

commit v8 on v6

--- a/solution.py
+++ b/solution.py
@@ -47,6 +47,8 @@
         self.order = order
         self.pc = self.c if order > 0 else 1 - self.c
         self.slot = self.x * self.nz + self.z
+        self.xs = [(self.x + i) % self.nx for i in range(self.nx)]
+        self.base = [x * 2 * self.nz + self.c for x in self.xs]
         self.mate = self.z + 1 - 2 * (self.z % 2)
         self.first = self.z % 2 == (0 if order > 0 else 1)
         self.far = (self.z + self.nz // 2) % self.nz
@@ -80,12 +82,12 @@
         to = self.device(self.x, self.mate, self.c)
         return self.remote(self.on, self.pin.at[self.passed], 5, self.ro.at[self.passed], to)
 
-    def in_copy(self, src, m, r):
-        return self.remote(src.at[r], self.gin.at[self.slot], 1, self.ri, self.device(r, m, self.c))
-
-    def out_copy(self, x, z):
-        to = self.device(x, z, self.c)
-        return self.remote(self.pout.at[x * self.nz + z], self.pin.at[self.z, self.x], 2, self.ro.at[self.z], to)
+    def in_copy(self, src, m, i):
+        return self.remote(src.at[self.xs[i]], self.gin.at[self.slot], 1, self.ri, (self.y, self.base[i] + 2 * m))
+
+    def out_copy(self, i, z):
+        to = (self.y, self.base[i] + 2 * z)
+        return self.remote(self.pout.at[self.xs[i] * self.nz + z], self.pin.at[self.z, self.x], 2, self.ro.at[self.z], to)
 
     def bk_copy(self, m):
         return self.remote(self.bkout.at[m], self.bkin.at[m], 3, self.rb.at[m], self.partner())
@@ -102,7 +104,7 @@
         @pl.when((m != self.far) & (m != self.passed))
         def _():
             for i in range(1, self.nx):
-                self.in_copy(self.s.at[m], m, (self.x + i) % self.nx).start()
+                self.in_copy(self.s.at[m], m, i).start()
 
             @pl.when(m == self.z)
             def _():
@@ -110,13 +112,13 @@
 
             @pl.when(m != self.z)
             def _():
-                self.in_copy(self.s.at[m], m, self.x).start()
+                self.in_copy(self.s.at[m], m, 0).start()
 
     def pass_in(self):
         self.give_copy().wait_recv()
         self.both[...] = self.s[self.passed] + self.given[...]
-        for r in range(self.nx):
-            self.in_copy(self.both, self.passed, r).start()
+        for i in range(self.nx):
+            self.in_copy(self.both, self.passed, i).start()
 
     def scan(self):
         slots = self.nx * self.nz
@@ -131,11 +133,12 @@
 
         @pl.loop(0, self.nz - 2)
         def _(e):
+            to = ring(SEND, e, self.z, self.nz)
             for i in range(self.nx):
-                self.out_copy((self.x + i) % self.nx, ring(SEND, e, self.z, self.nz)).start()
+                self.out_copy(i, to).start()
 
         for i in range(1, self.nx):
-            self.out_copy((self.x + i) % self.nx, self.z).start()
+            self.out_copy(i, self.z).start()
 
     def arrived(self, m, parts):
         part = self.pin.at[m, pl.ds(0, parts)]
@@ -183,9 +186,9 @@
     v_hbm,
     g_hbm,
     gain_ref,
-    dq_hbm,
-    dk_hbm,
-    dv_hbm,
+    dq_ref,
+    dk_ref,
+    dv_ref,
     dgain_ref,
     *scratch,
 ):
@@ -198,13 +201,13 @@
         return out
 
     q, k, v, g = take(4)
-    dq, dk, dv = take(3)
+    dq, dk, dv = dq_ref.at[0], dk_ref.at[0], dv_ref.at[0]
     scores, d_out, prior = take(3)
     out_loc, dk_loc, dv_loc = take(3)
     gtile, gin1, acc1, gin2, acc2, gin3, acc3, gin4 = take(8)
     bufs1, sems1 = take(11), take(6)
     bufs2, sems2 = take(11), take(6)
-    in_sem, out_sem, gsend, g1r, g2r, g3r, g4r = take(7)
+    in_sem, gsend, g1r, g2r, g3r, g4r = take(6)
 
     y = lax.axis_index("dp")
     ctx = lax.axis_index("ctx")
@@ -326,9 +329,6 @@
             dk_loc[h] = dkh
             dv_loc[h] = dvh
 
-    def store(ref, hbm, i, h):
-        return pltpu.make_async_copy(ref.at[:, col(h)], hbm.at[0, :, col(h)], out_sem.at[i])
-
     def pass_two(heads, states):
         ks, vs = columns(k, heads), columns(v, heads)
         dks, dvs = [dk_loc[h] for h in heads], [dv_loc[h] for h in heads]
@@ -338,9 +338,6 @@
         for h, dkh, dvh in zip(heads, dks, dvs):
             dk[:, col(h)] = dkh
             dv[:, col(h)] = dvh
-        for h in heads:
-            store(dk, dk_hbm, 1, h).start()
-            store(dv, dv_hbm, 2, h).start()
 
     ry, rx = HEADS // ny, HEADS // ny // nx
 
@@ -450,7 +447,6 @@
         def _():
             gain_step(1)
 
-    pltpu.make_async_copy(dq, dq_hbm.at[0], out_sem.at[0]).start()
     gain_step(2)
     two.scan()
     gain_step(3)
@@ -466,8 +462,6 @@
     for i in range(1, nz):
         g3_copy(i).wait_send()
     g4_copy().wait_send()
-    for i, (ref, hbm) in enumerate(((dq, dq_hbm), (dk, dk_hbm), (dv, dv_hbm))):
-        pltpu.make_async_copy(ref, hbm.at[0], out_sem.at[i]).wait()
 
 
 def hand_over(nz, a, b, c, gain, a_out, b_out, c_out, gain_out, gain_buf, sems):
@@ -516,7 +510,7 @@
         ]
 
     scratch = [
-        *[pltpu.VMEM((DIM, width), BF16)] * 7,
+        *[pltpu.VMEM((DIM, width), BF16)] * 4,
         *[pltpu.VMEM((HEADS, DIM, DIM), BF16)] * 3,
         *[pltpu.VMEM((HEADS, DIM, DIM), F32)] * 3,
         pltpu.VMEM((HEADS, 8, DIM), F32),
@@ -530,7 +524,6 @@
         *scan_scratch(),
         *scan_scratch(),
         pltpu.SemaphoreType.DMA((4,)),
-        pltpu.SemaphoreType.DMA((3,)),
         pltpu.SemaphoreType.DMA((4,)),
         pltpu.SemaphoreType.DMA((ny - 1,)),
         pltpu.SemaphoreType.DMA((nx - 1,)),
@@ -544,7 +537,7 @@
             functools.partial(kernel, (ny, nx, nz)),
             out_shape=(*[pltpu.VMEM(queries.shape, BF16)] * 3, pltpu.VMEM((rx, 8, DIM), F32)),
             in_specs=[pl.BlockSpec(memory_space=pl.ANY)] * 4 + [pl.BlockSpec(memory_space=pltpu.VMEM)],
-            out_specs=[pl.BlockSpec(memory_space=pl.ANY)] * 3 + [pl.BlockSpec(memory_space=pltpu.VMEM)],
+            out_specs=[pl.BlockSpec(memory_space=pltpu.VMEM)] * 4,
             scratch_shapes=scratch,
             compiler_params=pltpu.CompilerParams(
                 collective_id=0, has_side_effects=True, vmem_limit_bytes=62 * 1024 * 1024

time: 73.7 us -> 73.5 us (level)
  no operation moved by 1% of the time
where the time goes in v8:
time: 73.5 us; the launch traced here: 73.3 us
  Pallas kernels  72.7 us (99%)
    pallas_call x1, Pallas kernels, body(): pl.pallas_call(functools.partial(kernel, (ny, nx, nz)), out_shape=(*[pltp...  70.9 us
    pallas_call x1, Pallas kernels, body(): pl.pallas_call(functools.partial(hand_over, nz), out_shape=(rows, rows, r...  1.76 us

profile of v8, /device:TPU:1, one launch (start us, length us, event | category | flops | bytes accessed | tf_op | source)
XLA Modules:
  0.0 73.3 jit_solution(1438648400149058173)
XLA Ops:
  0.6 70.9 %shard_map.84 = (bf16[1,128,2048]{2,1,0:T(8,128)(2,1)S(1)}, bf16[1,128,2048]{2,1,0:T(8,128)(2,1)S(1)}, bf16[1,128,2048]{2,1,0:T(8,128)(2,1)S(1)}, f32[1,8,128]{2,1,0:T(8,128)S(1)}) custom-call(bf16[1,128,2048]{2,1,0:T(8,128)(2,1)} %q_hbm.1, bf16[1,128,2048]{2,1,0:T(8,128)(2,1)} %k_hbm.1, bf16[1,128,2048]{2,1,0:T(8,128)(2,1)} %v_hbm.1, ...), custom_call_target="tpu_custom_call" | custom-call | tf_op jit(solution)/shard_map/pallas_call | solution.py:536
  71.6 1.8 %shard_map.85 = (bf16[1,128,2048]{2,1,0:T(8,128)(2,1)}, bf16[1,128,2048]{2,1,0:T(8,128)(2,1)}, bf16[1,128,2048]{2,1,0:T(8,128)(2,1)}, f32[1,8]{1,0:T(1,128)}) custom-call(bf16[1,128,2048]{2,1,0:T(8,128)(2,1)S(1)} %get-tuple-element.12.a, bf16[1,128,2048]{2,1,0:T(8,128)(2,1)S(1)} %get-tuple-element.13.b, bf16[1,128,2048]{2,1,0:T(8,128)(2,1)S(1)} %get-tuple-element.14.c, ...), custom_call_target="tpu_custom_call" | custom-call | tf_op jit(solution)/shard_map/pallas_call | solution.py:547

commit v9 on v8

--- a/solution.py
+++ b/solution.py
@@ -219,7 +219,13 @@
     def device(y_, x_, z_, c_):
         return (y_, (x_ * nz + z_) * 2 + c_)
 
-    loads = [pltpu.make_async_copy(src.at[0], dst, in_sem.at[i]) for i, (src, dst) in enumerate(((k_hbm, k), (v_hbm, v), (q_hbm, q), (g_hbm, g)))]
+    def load(src, dst, first, i):
+        part = pl.ds(pl.multiple_of(first * DIM, HALF * DIM), HALF * DIM)
+        return pltpu.make_async_copy(src.at[0, :, part], dst.at[:, part], in_sem.at[i])
+
+    loads = [load(src, dst, (1 - c) * HALF, i) for i, (src, dst) in enumerate(((k_hbm, k), (v_hbm, v)))]
+    loads += [load(src, dst, c * HALF, 2 + i) for i, (src, dst) in enumerate(((k_hbm, k), (v_hbm, v)))]
+    loads += [pltpu.make_async_copy(src.at[0], dst, in_sem.at[4 + i]) for i, (src, dst) in enumerate(((q_hbm, q), (g_hbm, g)))]
     for load in loads:
         load.start()
 
@@ -275,14 +281,18 @@
         for u in range(4):
             one.exch_copy(place(i + u)).start()
 
+    loads[2].wait()
+    loads[3].wait()
+
     for i in range(0, HALF, 4):
         local_states([mine + place(i + u) for u in range(4)])
+        if i == 4:
+            one.pass_in()
         for u in range(4):
             one.add_chip(place(i + u))
-    one.pass_in()
-
-    loads[2].wait()
-    loads[3].wait()
+
+    loads[4].wait()
+    loads[5].wait()
 
     keep = lax.broadcasted_iota(jnp.int32, (DIM, DIM), 0) >= lax.broadcasted_iota(jnp.int32, (DIM, DIM), 1)
 
@@ -406,7 +416,7 @@
             def _():
                 last(arrival(e - LAG - SUM_LAG))
 
-            @pl.when(e == HALF + LAG)
+            @pl.when(e == HALF + LAG - 1)
             def _():
                 final()
 
@@ -523,7 +533,7 @@
         pltpu.VMEM((rx, 8, DIM), F32),
         *scan_scratch(),
         *scan_scratch(),
-        pltpu.SemaphoreType.DMA((4,)),
+        pltpu.SemaphoreType.DMA((6,)),
         pltpu.SemaphoreType.DMA((4,)),
         pltpu.SemaphoreType.DMA((ny - 1,)),
         pltpu.SemaphoreType.DMA((nx - 1,)),

time: 73.5 us -> 75.6 us (1.029)
  Pallas kernels: 72.7 us -> 74.8 us
    pallas_call x1, Pallas kernels: 70.9 us -> 73.1 us  [body(): pl.pallas_call(functools.partial(kernel, (ny, nx, nz)), out_shape=(*[pltp...]
where the time goes in v9:
time: 75.6 us; the launch traced here: 75.5 us
  Pallas kernels  74.8 us (99%)
    pallas_call x1, Pallas kernels, body(): pl.pallas_call(functools.partial(kernel, (ny, nx, nz)), out_shape=(*[pltp...  73.1 us
    pallas_call x1, Pallas kernels, body(): pl.pallas_call(functools.partial(hand_over, nz), out_shape=(rows, rows, r...  1.76 us

profile of v9, /device:TPU:1, one launch (start us, length us, event | category | flops | bytes accessed | tf_op | source)
XLA Modules:
  0.0 75.5 jit_solution(2994208479227853274)
XLA Ops:
  0.6 73.1 %shard_map.84 = (bf16[1,128,2048]{2,1,0:T(8,128)(2,1)S(1)}, bf16[1,128,2048]{2,1,0:T(8,128)(2,1)S(1)}, bf16[1,128,2048]{2,1,0:T(8,128)(2,1)S(1)}, f32[1,8,128]{2,1,0:T(8,128)S(1)}) custom-call(bf16[1,128,2048]{2,1,0:T(8,128)(2,1)} %q_hbm.1, bf16[1,128,2048]{2,1,0:T(8,128)(2,1)} %k_hbm.1, bf16[1,128,2048]{2,1,0:T(8,128)(2,1)} %v_hbm.1, ...), custom_call_target="tpu_custom_call" | custom-call | tf_op jit(solution)/shard_map/pallas_call | solution.py:546
  73.7 1.8 %shard_map.85 = (bf16[1,128,2048]{2,1,0:T(8,128)(2,1)}, bf16[1,128,2048]{2,1,0:T(8,128)(2,1)}, bf16[1,128,2048]{2,1,0:T(8,128)(2,1)}, f32[1,8]{1,0:T(1,128)}) custom-call(bf16[1,128,2048]{2,1,0:T(8,128)(2,1)S(1)} %get-tuple-element.12.a, bf16[1,128,2048]{2,1,0:T(8,128)(2,1)S(1)} %get-tuple-element.13.b, bf16[1,128,2048]{2,1,0:T(8,128)(2,1)S(1)} %get-tuple-element.14.c, ...), custom_call_target="tpu_custom_call" | custom-call | tf_op jit(solution)/shard_map/pallas_call | solution.py:557
